TPU v7x, 32 devices: a whole 2x2x4 slice. The times are simulated.
32 devices in a mesh: mod: 2 (over x), dp: 16 (over z, y, core).
Axes of the slice: x: 2, y: 2, z: 4, core: 2. Of those that a mesh axis runs over, the one named last changes fastest.
Arguments:
- layer_rows: bfloat16 [2, 16384, 768], P('mod', 'dp'), may hold values from -6 to 6
- cotangent: bfloat16 [2, 16384, 768], P('mod', 'dp'), may hold values from -6 to 6
- row_live: int32 [2, 16384], P(None, 'dp'), may hold values from 0 to 1, as said below
- partner: int32 [16, 16], P('dp'), may hold values from 0 to 15, as said below
- w_qkv: bfloat16 [768, 2304], replicated, may hold values from -0.21875 to 0.21875
- b_qv: float32 [2, 768], replicated, may hold values from -1.8 to 1.8
- w_out: bfloat16 [768, 768], replicated, may hold values from -0.875 to 0.875
- norm_gains: float32 [2, 768], replicated, may hold values from 0.5 to 1.5
- bias_rows: float32 [4, 768], replicated, may hold values from -1.8 to 1.8
- w_in: bfloat16 [768, 3072], replicated, may hold values from -0.21875 to 0.21875
- b_in: float32 [3072], replicated, may hold values from -1.8 to 1.8
- w_back: bfloat16 [3072, 768], replicated, may hold values from -0.15625 to 0.15625
Outputs:
- output: bfloat16 [2, 16384, 768], P('mod', 'dp')
- grad_rows: bfloat16 [2, 16384, 768], P('mod', 'dp')
- grad_w_qkv: float32 [768, 2304], P('dp')
- grad_b_qv: float32 [2, 768], P(None, 'dp')
- grad_w_out: float32 [768, 768], P('dp')
- grad_gains: float32 [2, 768], P(None, 'dp')
- grad_biases: float32 [4, 768], P(None, 'dp')
- grad_w_in: float32 [768, 3072], P('dp')
- grad_b_in: float32 [3072], P('dp')
- grad_w_back: float32 [3072, 768], P('dp')
Inputs may be any that keep to these rules, and one draw needn't show every extreme that they name: `row_live`: within each pair and modality the live rows are the first ones of its 64 slots, at least one; the first pair of every index of dp is live in all its rows of both modalities. Each row partner[g] is a permutation of the 16 region slots of index g of dp.
All inputs are finite; a program needn't handle non-finite values.
Results may differ from a plain program's by a relative error of at most 0.015.
Values may be sent and summed in bfloat16 or wider, within the bound.
No kernel may reach another device: no remote copies, remote signals or barrier semaphores. Data moves between devices by JAX's collectives and lax.ppermute only.
A program may use at most 192 MiB of HBM per device.

v0:
```python
import functools

import jax
import jax.numpy as jnp
from jax import lax
from jax.experimental import pallas as pl
from jax.experimental.pallas import tpu as pltpu
from jax.sharding import PartitionSpec as P

HEADS = 12
EPSILON = 1e-12
F32 = jnp.float32
BF16 = jnp.bfloat16
VMEM_LIMIT = 56 * 2**20


def dot(left, right, left_dim=1, right_dim=0):
    return lax.dot_general(
        left, right, (((left_dim,), (right_dim,)), ((), ())), preferred_element_type=F32
    )


def flipped(value, axis, mask):
    pairs = [(source, source ^ mask) for source in range(lax.axis_size(axis))]
    return lax.ppermute(value, axis, pairs)


def params(limit=VMEM_LIMIT):
    return pltpu.CompilerParams(vmem_limit_bytes=limit)


def kept_slot(scalars, pair, half):
    groups = 2 * half
    side = scalars[groups]
    place = side * half + pair
    return jnp.where(side == 0, place, scalars[place])


def sent_slot(scalars, pair, half):
    groups = 2 * half
    side = scalars[groups]
    place = (1 - side) * half + pair
    return jnp.where(side == 0, place, scalars[place])


ANY = pl.BlockSpec(memory_space=pl.ANY)


def call(kernel, scalars, operands, in_specs, out_specs, out_shape, grid, name, work, **more):
    after = list(more.get("after", ()))
    into = list(more.get("into", ()))
    scratch = list(more.get("scratch", ()))
    taken, spare = len(operands), len(into) + len(after)

    def wrapped(scalars_ref, *refs):
        kernel(scalars_ref, *refs[:taken], *refs[taken + spare :])

    return pl.pallas_call(
        wrapped,
        grid_spec=pltpu.PrefetchScalarGridSpec(
            num_scalar_prefetch=1,
            grid=grid,
            in_specs=list(in_specs) + [ANY] * spare,
            out_specs=out_specs,
            scratch_shapes=scratch,
        ),
        out_shape=out_shape,
        input_output_aliases={
            1 + taken + i: i + more.get("into_first", 0) for i in range(len(into))
        },
        compiler_params=params(more.get("limit", VMEM_LIMIT)),
        cost_estimate=pl.CostEstimate(
            flops=int(work), bytes_accessed=more.get("moved", 2**20), transcendentals=0
        ),
        name=name,
    )(scalars, *operands, *into, *after)


def gather_sent(scalars, rows, half, first, count, after=()):
    slot_rows, width = rows.shape[1:]

    def kernel(scalars_ref, rows_ref, out, sems):
        copies = [
            pltpu.make_async_copy(
                rows_ref.at[sent_slot(scalars_ref, first + i, half)], out.at[i], sems.at[i]
            )
            for i in range(count)
        ]
        for copy in copies:
            copy.start()
        for copy in copies:
            copy.wait()

    shape = (count, slot_rows, width)
    return call(
        kernel,
        scalars,
        [rows],
        [ANY],
        pl.BlockSpec(shape, lambda i, s: (0, 0, 0)),
        jax.ShapeDtypeStruct(shape, rows.dtype),
        (1,),
        "gather_sent",
        1e6,
        scratch=[pltpu.SemaphoreType.DMA((count,))],
        after=after,
        limit=8 * 2**20,
    )


def scatter_home(scalars, kept, back, half, after=()):
    slot_rows, width = kept.shape[1:]

    def kernel(scalars_ref, kept_ref, back_ref, out, sems):
        copies = []
        for i in range(half):
            copies.append(
                pltpu.make_async_copy(
                    kept_ref.at[i], out.at[kept_slot(scalars_ref, i, half)], sems.at[0, i]
                )
            )
            copies.append(
                pltpu.make_async_copy(
                    back_ref.at[i], out.at[sent_slot(scalars_ref, i, half)], sems.at[1, i]
                )
            )
        for copy in copies:
            copy.start()
        for copy in copies:
            copy.wait()

    shape = (2 * half, slot_rows, width)
    return call(
        kernel,
        scalars,
        [kept, back],
        [ANY, ANY],
        pl.BlockSpec(shape, lambda i, s: (0, 0, 0)),
        jax.ShapeDtypeStruct(shape, kept.dtype),
        (1,),
        "scatter_home",
        1e6,
        scratch=[pltpu.SemaphoreType.DMA((2, half))],
        after=after,
        limit=8 * 2**20,
    )


def split_heads(value):
    low = lax.broadcasted_iota(jnp.int32, value.shape, 1) < value.shape[1] // 2
    zero = jnp.zeros_like(value)
    return jnp.concatenate([jnp.where(low, value, zero), jnp.where(low, zero, value)], 0)


def side_by_side(value):
    rows = value.shape[0] // 2
    return jnp.concatenate([value[:rows], value[rows:]], 1)


def row_sum(value):
    return jnp.sum(value, axis=0, keepdims=True)


def normal_form(value):
    centered = value - jnp.mean(value, axis=-1, keepdims=True)
    root = lax.rsqrt(jnp.mean(centered * centered, axis=-1, keepdims=True) + EPSILON)
    return centered * root, root


def normal_back(lifted, normed, root):
    return root * (
        lifted
        - jnp.mean(lifted, axis=-1, keepdims=True)
        - normed * jnp.mean(lifted * normed, axis=-1, keepdims=True)
    )


def whole(array):
    return pl.BlockSpec(
        array.shape, lambda *_: (0,) * array.ndim, pipeline_mode=pl.Buffered(1)
    )


def attention_forward(
    scalars, rows, received, live, weights, first, half, into=(), after=()
):
    w_qkv, b_qv, w_out, norm_gains, bias_rows = weights
    slot_rows, width = rows.shape[1:]
    pairs = received.shape[0]
    length = 2 * slot_rows
    duo = 2 * width // HEADS
    blocks = width // duo
    score_scale = (width // HEADS) ** (-0.5)

    def kernel(
        scalars_ref,
        kept_a,
        kept_b,
        got,
        live_ref,
        w_qkv_ref,
        b_qv_ref,
        w_out_ref,
        gains_ref,
        biases_ref,
        joined_out,
        mixed_out,
        probs_out,
        context_out,
        normed_out,
        root_out,
    ):
        joined = jnp.concatenate([kept_a[0], got[0], kept_b[0], got[1]], 0)
        joined_out[...] = joined
        mixed = dot(joined, w_qkv_ref[...])
        queries = (mixed[:, :width] + b_qv_ref[0:1, :]).astype(BF16)
        queries = (queries.astype(F32) * score_scale).astype(BF16)
        keys = mixed[:, width : 2 * width].astype(BF16)
        values = (mixed[:, 2 * width :] + b_qv_ref[1:2, :]).astype(BF16)
        mixed_out[:, :width] = queries
        mixed_out[:, width : 2 * width] = keys
        mixed_out[:, 2 * width :] = values
        contexts = []
        for pair in range(2):
            seen = live_ref[pair] > 0
            span = slice(pair * length, (pair + 1) * length)
            heads = []
            for block in range(blocks):
                cols = slice(block * duo, (block + 1) * duo)
                scores = dot(split_heads(queries[span, cols]), keys[span, cols], 1, 1)
                scores = jnp.where(seen, scores, -1e30)
                powered = jnp.exp(scores - jnp.max(scores, axis=-1, keepdims=True))
                low_probs = powered * (1.0 / jnp.sum(powered, axis=-1, keepdims=True))
                low_probs = low_probs.astype(BF16)
                probs_out[pair, block] = low_probs
                heads.append(
                    dot(side_by_side(low_probs), split_heads(values[span, cols])).astype(BF16)
                )
            contexts.append(jnp.concatenate(heads, 1))
        context = jnp.concatenate(contexts, 0)
        context_out[...] = context
        pre_one = joined.astype(F32) + dot(context, w_out_ref[...]) + biases_ref[0:1, :]
        normed, root = normal_form(pre_one)
        normed_out[...] = normed.astype(BF16)
        root_out[...] = jnp.broadcast_to(root, root_out.shape)

    start = first // 2

    def by_rows(columns):
        return pl.BlockSpec((2 * length, columns), lambda i, s: (start + i, 0))

    slot = (1, slot_rows, width)
    total = half * length
    return call(
        kernel,
        scalars,
        [rows, rows, received, live, w_qkv, b_qv, w_out, norm_gains, bias_rows],
        [
            pl.BlockSpec(slot, lambda i, s: (kept_slot(s, first + 2 * i, half), 0, 0)),
            pl.BlockSpec(slot, lambda i, s: (kept_slot(s, first + 2 * i + 1, half), 0, 0)),
            pl.BlockSpec((2, slot_rows, width), lambda i, s: (i, 0, 0)),
            pl.BlockSpec((2, 1, length), lambda i, s: (start + i, 0, 0)),
            whole(w_qkv),
            whole(b_qv),
            whole(w_out),
            whole(norm_gains),
            whole(bias_rows),
        ],
        [
            by_rows(width),
            by_rows(3 * width),
            pl.BlockSpec((2, blocks, 2 * length, length), lambda i, s: (start + i, 0, 0, 0)),
            by_rows(width),
            by_rows(width),
            by_rows(128),
        ],
        [
            jax.ShapeDtypeStruct((total, width), BF16),
            jax.ShapeDtypeStruct((total, 3 * width), BF16),
            jax.ShapeDtypeStruct((half, blocks, 2 * length, length), BF16),
            jax.ShapeDtypeStruct((total, width), BF16),
            jax.ShapeDtypeStruct((total, width), BF16),
            jax.ShapeDtypeStruct((total, 128), F32),
        ],
        (pairs // 2,),
        "attention_forward",
        pairs * length * width * width * 10,
        into=into,
        after=after,
        moved=12 * 2**20,
    )


def spread(grad, out_pairs, scalars_ref, base, shard, first_row, places):
    core = scalars_ref[base + 1]
    for j in range(places):
        row = (first_row ^ j) * 2
        for out, which in ((out_pairs[0], 1 - core), (out_pairs[1], core)):
            out[j] = grad[pl.ds(pl.multiple_of((row + which) * shard, 16), shard), :]


def feed_forward(scalars, normed, cot, far_cot, weights, half, shards, base, after=()):
    w_in, b_in, w_back, norm_gains, bias_rows = weights
    slot_rows, width = cot.shape[1:]
    inner_width = w_in.shape[1]
    length = 2 * slot_rows
    rows = 2 * length
    height = half * length
    steps = half // 2
    chunk = 768
    chunks = inner_width // chunk
    shard = inner_width // shards
    places = shards // 2
    part = 4 * shard
    parts = inner_width // part
    left = width // 2

    def kernel(
        scalars_ref,
        normed_ref,
        cot_a,
        cot_b,
        cot_far,
        w_in_hbm,
        b_in_ref,
        w_back_hbm,
        gains_ref,
        biases_ref,
        slope_out,
        branch_out,
        kept_out,
        far_out,
        sums_out,
        send_a,
        keep_a,
        send_b,
        keep_b,
        w_in_ref,
        w_back_ref,
        held,
        acts,
        branches,
        grad_a,
        grad_b,
        sems,
    ):
        step = pl.program_id(0)

        def fetch_in(j):
            cols = pl.ds(j * chunk, chunk)
            return pltpu.make_async_copy(
                w_in_hbm.at[:, cols], w_in_ref.at[:, cols], sems.at[0, j]
            )

        def fetch_back(j):
            cols = pl.ds(j * chunk, chunk)
            return pltpu.make_async_copy(w_back_hbm.at[cols], w_back_ref.at[cols], sems.at[1, j])

        @pl.when(step == 0)
        def _():
            sums_out[...] = jnp.zeros_like(sums_out)
            for j in range(chunks):
                fetch_in(j).start()
                fetch_back(j).start()

        def close(pre_two, row):
            scaled, root = normal_form(pre_two)
            output = (scaled * gains_ref[1:2, :] + biases_ref[3:4, :]).astype(BF16)
            for i in range(2):
                kept_out[i] = output[i * length : i * length + slot_rows]
                far_out[i] = output[i * length + slot_rows : (i + 1) * length]
            here = jnp.concatenate([cot_a[0], cot_far[0], cot_b[0], cot_far[1]], 0).astype(F32)
            d_two = normal_back(here * gains_ref[1:2, :], scaled, root)
            low = d_two.astype(BF16)
            branch_out[...] = low
            branches[pl.ds(row, rows)] = low
            return jnp.concatenate([row_sum(here * scaled), row_sum(here), row_sum(d_two)], 0)

        def forward(first):
            hidden = normed_ref[...].astype(F32) * gains_ref[0:1, :] + biases_ref[1:2, :]
            low_hidden = hidden.astype(BF16)
            total = hidden + biases_ref[2:3, :]
            for j in range(chunks):
                cols = slice(j * chunk, (j + 1) * chunk)
                if first:
                    fetch_in(j).wait()
                inner = dot(low_hidden, w_in_ref[:, cols]) + b_in_ref[:, cols]
                normal = 0.5 + 0.5 * lax.erf(inner * (0.5**0.5))
                low_act = (inner * normal).astype(BF16)
                density = jnp.exp(inner * inner * -0.5) * 0.3989422804014327
                acts[pl.ds(step * rows, rows), cols] = low_act
                slope_out[:, cols] = (normal + inner * density).astype(BF16)
                if first:
                    fetch_back(j).wait()
                total = total + dot(low_act, w_back_ref[cols, :])
            return total

        @pl.when(step == 0)
        def _():
            held[...] = forward(True)

        @pl.when((step > 0) & (step < steps))
        def _():
            before = held[...]
            held[...] = forward(False)
            sums_out[0:3, :] += close(before, (step - 1) * rows)

        @pl.when(step == steps)
        def _():
            sums_out[0:3, :] += close(held[...], (step - 1) * rows)

        @pl.when(step >= steps)
        def _():
            start = pl.multiple_of((step - steps) * part, 128)
            grad = dot(acts[:, pl.ds(start, part)], branches[...], 0, 0).astype(BF16)
            grad_a[...] = grad[:, :left]
            grad_b[...] = grad[:, left:]
            first_row = scalars_ref[base + 2] & 1
            spread(grad_a, (send_a, keep_a), scalars_ref, base, shard, first_row, 2)
            spread(grad_b, (send_b, keep_b), scalars_ref, base, shard, first_row, 2)

    def ahead(i):
        return jnp.minimum(i, steps - 1)

    def behind(i):
        return jnp.clip(i - 1, 0, steps - 1)

    def slot(j):
        return pl.BlockSpec(
            (1, slot_rows, width), lambda i, s: (kept_slot(s, 2 * behind(i) + j, half), 0, 0)
        )

    duo = pl.BlockSpec((2, slot_rows, width), lambda i, s: (behind(i), 0, 0))
    grads = []
    for columns in (left, left, width - left, width - left):
        grads.append(
            pl.BlockSpec(
                (2, shard, columns),
                lambda i, s: ((s[base + 2] >> 1) ^ jnp.maximum(i - steps, 0), 0, 0),
            )
        )
    return call(
        kernel,
        scalars,
        [normed, cot, cot, far_cot, w_in, b_in, w_back, norm_gains, bias_rows],
        [
            pl.BlockSpec((rows, width), lambda i, s: (ahead(i), 0)),
            slot(0),
            slot(1),
            duo,
            ANY,
            whole(b_in),
            ANY,
            whole(norm_gains),
            whole(bias_rows),
        ],
        [
            pl.BlockSpec((rows, inner_width), lambda i, s: (ahead(i), 0)),
            pl.BlockSpec((rows, width), lambda i, s: (behind(i), 0)),
            duo,
            duo,
            pl.BlockSpec((8, width), lambda i, s: (0, 0)),
        ]
        + grads,
        [
            jax.ShapeDtypeStruct((height, inner_width), BF16),
            jax.ShapeDtypeStruct((height, width), BF16),
            jax.ShapeDtypeStruct((half, slot_rows, width), BF16),
            jax.ShapeDtypeStruct((half, slot_rows, width), BF16),
            jax.ShapeDtypeStruct((8, width), F32),
            jax.ShapeDtypeStruct((places, shard, left), BF16),
            jax.ShapeDtypeStruct((places, shard, left), BF16),
            jax.ShapeDtypeStruct((places, shard, width - left), BF16),
            jax.ShapeDtypeStruct((places, shard, width - left), BF16),
        ],
        (steps + parts,),
        "feed_forward",
        height * width * inner_width * 6,
        after=after,
        scratch=[
            pltpu.VMEM((width, inner_width), BF16),
            pltpu.VMEM((inner_width, width), BF16),
            pltpu.VMEM((rows, width), F32),
            pltpu.VMEM((height, inner_width), BF16),
            pltpu.VMEM((height, width), BF16),
            pltpu.VMEM((part, left), BF16),
            pltpu.VMEM((part, width - left), BF16),
            pltpu.SemaphoreType.DMA((2, chunks)),
        ],
        moved=28 * 2**20,
    )


def feed_backward(scalars, branch, slope, normed, root, context, weights, shards, base, after=()):
    w_in, w_back, norm_gains, bias_rows = weights
    total, width = branch.shape
    inner_width = slope.shape[1]
    chunk = 768
    steps = inner_width // chunk
    turn = steps // 2
    shard = width // shards
    places = shards // 2
    piece = 128

    def kernel(
        scalars_ref,
        branch_ref,
        slope_ref,
        normed_ref,
        root_ref,
        context_ref,
        w_in_ref,
        w_back_ref,
        gains_ref,
        biases_ref,
        low_attn_out,
        sums_out,
        inner_sum_out,
        send_a,
        keep_a,
        send_b,
        keep_b,
        send_out,
        keep_out,
        held,
        low_hidden,
        grad,
    ):
        step = pl.program_id(0)
        place = scalars_ref[base + 2]

        @pl.when(step == 0)
        def _():
            hidden = normed_ref[...].astype(F32) * gains_ref[0:1, :] + biases_ref[1:2, :]
            low_hidden[...] = hidden.astype(BF16)
            held[...] = branch_ref[...].astype(F32)

        sums = jnp.zeros((1, chunk), F32)
        lows = []
        for r in range(0, total, 256):
            span = slice(r, r + 256)
            d_inner = dot(branch_ref[span], w_back_ref[...], 1, 1) * slope_ref[span].astype(F32)
            sums = sums + row_sum(d_inner)
            low = d_inner.astype(BF16)
            lows.append(low)
            held[span] += dot(low, w_in_ref[...], 1, 1)
        inner_sum_out[...] = jnp.broadcast_to(sums, inner_sum_out.shape)
        grad[...] = dot(low_hidden[...], jnp.concatenate(lows, 0), 0, 0).astype(BF16)

        @pl.when(step < turn)
        def _():
            spread(grad, (send_a, keep_a), scalars_ref, base, shard, place, places)

        @pl.when(step >= turn)
        def _():
            spread(grad, (send_b, keep_b), scalars_ref, base, shard, place, places)

        @pl.when(step == steps - 1)
        def _():
            sums = [jnp.zeros((1, width), F32)] * 3
            lows = []
            for i in range(total // piece):
                span = slice(i * piece, (i + 1) * piece)
                d_hidden, scaled = held[span], normed_ref[span].astype(F32)
                d_one = normal_back(d_hidden * gains_ref[0:1, :], scaled, root_ref[span, 0:1])
                lows.append(d_one.astype(BF16))
                low_attn_out[span] = lows[-1]
                for j, term in enumerate((d_hidden * scaled, d_hidden, d_one)):
                    sums[j] = sums[j] + row_sum(term)
            sums_out[...] = jnp.concatenate(sums + [jnp.zeros((5, width), F32)], 0)
            grad[:, :width] = dot(context_ref[...], jnp.concatenate(lows, 0), 0, 0).astype(BF16)
            spread(grad, (send_out, keep_out), scalars_ref, base, shard, place, places)

    half_a = pl.BlockSpec((places, shard, chunk), lambda i, s: (0, 0, jnp.minimum(i, turn - 1)))
    half_b = pl.BlockSpec((places, shard, chunk), lambda i, s: (0, 0, jnp.maximum(i - turn, 0)))
    outer = pl.BlockSpec((places, shard, width), lambda i, s: (0, 0, 0))
    shape_a = jax.ShapeDtypeStruct((places, shard, turn * chunk), BF16)
    shape_b = jax.ShapeDtypeStruct((places, shard, inner_width - turn * chunk), BF16)
    shape_out = jax.ShapeDtypeStruct((places, shard, width), BF16)
    return call(
        kernel,
        scalars,
        [branch, slope, normed, root, context, w_in, w_back, norm_gains, bias_rows],
        [
            whole(branch),
            pl.BlockSpec((total, chunk), lambda i, s: (0, i)),
            whole(normed),
            whole(root),
            whole(context),
            pl.BlockSpec((width, chunk), lambda i, s: (0, i)),
            pl.BlockSpec((chunk, width), lambda i, s: (i, 0)),
            whole(norm_gains),
            whole(bias_rows),
        ],
        [
            pl.BlockSpec((total, width), lambda i, s: (0, 0)),
            pl.BlockSpec((8, width), lambda i, s: (0, 0)),
            pl.BlockSpec((8, chunk), lambda i, s: (0, i)),
            half_a,
            half_a,
            half_b,
            half_b,
            outer,
            outer,
        ],
        [
            jax.ShapeDtypeStruct((total, width), BF16),
            jax.ShapeDtypeStruct((8, width), F32),
            jax.ShapeDtypeStruct((8, inner_width), F32),
            shape_a,
            shape_a,
            shape_b,
            shape_b,
            shape_out,
            shape_out,
        ],
        (steps,),
        "feed_backward",
        total * width * inner_width * 6,
        after=after,
        scratch=[
            pltpu.VMEM((total, width), F32),
            pltpu.VMEM((total, width), BF16),
            pltpu.VMEM((width, chunk), BF16),
        ],
        moved=26 * 2**20,
    )


def attention_backward(scalars, kept, weights, part, parts, shards, base, into=(), after=()):
    low_attn, mixed, probs, joined = kept
    w_out, w_qkv = weights
    total, width = low_attn.shape
    pairs, blocks, _, length = probs.shape
    duo = width // blocks
    slot_rows = length // 2
    score_scale = (width // HEADS) ** (-0.5)
    steps = pairs // 2 // parts
    start = part * steps
    last = part == parts - 1
    before = start * 2 * length
    shard = width // shards
    places = shards // 2
    earlier = [into[0]] if last else []

    def kernel(
        scalars_ref,
        low_attn_ref,
        mixed_ref,
        probs_ref,
        w_out_ref,
        w_qkv_ref,
        *refs,
    ):
        if last:
            joined_ref, earlier_ref = refs[:2]
            refs = refs[2:]
        d_mixed_out, kept_out, far_out, sums_out = refs[:4]
        step = pl.program_id(0)

        @pl.when(step == 0)
        def _():
            sums_out[...] = jnp.zeros_like(sums_out)

        d_context = dot(low_attn_ref[...], w_out_ref[...], 1, 1).astype(BF16)
        for pair in range(2):
            span = slice(pair * length, (pair + 1) * length)
            for block in range(blocks):
                cols = slice(block * duo, (block + 1) * duo)
                key_cols = slice(width + block * duo, width + (block + 1) * duo)
                value_cols = slice(2 * width + block * duo, 2 * width + (block + 1) * duo)
                queries = split_heads(mixed_ref[span, cols])
                keys = mixed_ref[span, key_cols]
                values = mixed_ref[span, value_cols]
                d_heads = split_heads(d_context[span, cols])
                low_probs = probs_ref[pair, block]
                wide = low_probs.astype(F32)
                d_probs = dot(d_heads, values, 1, 1)
                d_scores = wide * (d_probs - jnp.sum(wide * d_probs, axis=-1, keepdims=True))
                d_scores = d_scores.astype(BF16)
                d_queries = dot(side_by_side(d_scores), split_heads(keys)) * score_scale
                d_mixed_out[span, cols] = d_queries.astype(BF16)
                d_mixed_out[span, key_cols] = dot(d_scores, queries, 0, 0).astype(BF16)
                d_mixed_out[span, value_cols] = dot(low_probs, d_heads, 0, 0).astype(BF16)
        d_mixed = d_mixed_out[...]
        sums_out[0:1, :] += row_sum(d_mixed[:, :width].astype(F32))
        sums_out[1:2, :] += row_sum(d_mixed[:, 2 * width :].astype(F32))
        d_rows = low_attn_ref[...].astype(F32) + dot(d_mixed, w_qkv_ref[...], 1, 1)
        d_rows = d_rows.astype(BF16)
        for i in range(2):
            kept_out[i] = d_rows[i * length : i * length + slot_rows]
            far_out[i] = d_rows[i * length + slot_rows : (i + 1) * length]
        if last:
            grads, (held, grad) = refs[4:10], refs[10:]
            held[pl.ds(step * 2 * length, 2 * length)] = d_mixed

            @pl.when(step == steps - 1)
            def _():
                for i in range(3):
                    cols = slice(i * width, (i + 1) * width)
                    total_grad = dot(joined_ref[:before], earlier_ref[:, cols], 0, 0)
                    total_grad = total_grad + dot(joined_ref[before:], held[:, cols], 0, 0)
                    grad[...] = total_grad.astype(BF16)
                    spread(
                        grad,
                        grads[2 * i : 2 * i + 2],
                        scalars_ref,
                        base,
                        shard,
                        scalars_ref[base + 2],
                        places,
                    )

    def by_rows(columns):
        return pl.BlockSpec((2 * length, columns), lambda i, s: (start + i, 0))

    two = pl.BlockSpec((2, slot_rows, width), lambda i, s: (start + i, 0, 0))
    operands = [low_attn, mixed, probs, w_out, w_qkv]
    in_specs = [
        by_rows(width),
        by_rows(3 * width),
        pl.BlockSpec((2, blocks, 2 * length, length), lambda i, s: (start + i, 0, 0, 0)),
        whole(w_out),
        whole(w_qkv),
    ]
    out_specs = [by_rows(3 * width), two, two, pl.BlockSpec((8, width), lambda i, s: (0, 0))]
    out_shape = [
        jax.ShapeDtypeStruct((total, 3 * width), BF16),
        jax.ShapeDtypeStruct((pairs, slot_rows, width), BF16),
        jax.ShapeDtypeStruct((pairs, slot_rows, width), BF16),
        jax.ShapeDtypeStruct((8, width), F32),
    ]
    scratch = []
    if last:
        operands += [joined, into[0]]
        in_specs += [
            whole(joined),
            pl.BlockSpec((before, 3 * width), lambda i, s: (0, 0), pipeline_mode=pl.Buffered(1)),
        ]
        out_specs[0] = by_rows(3 * width)
        out_specs += [pl.BlockSpec((places, shard, width), lambda i, s: (0, 0, 0))] * 6
        out_shape += [jax.ShapeDtypeStruct((places, shard, width), BF16)] * 6
        scratch = [
            pltpu.VMEM((steps * 2 * length, 3 * width), BF16),
            pltpu.VMEM((width, width), BF16),
        ]
        out_specs[0] = pl.BlockSpec((2 * length, 3 * width), lambda i, s: (0, 0))
        out_shape[0] = jax.ShapeDtypeStruct((2 * length, 3 * width), BF16)
    return call(
        kernel,
        scalars,
        operands,
        in_specs,
        out_specs,
        out_shape,
        (steps,),
        "attention_backward",
        total // parts * width * width * 20,
        into=into[1:],
        into_first=1,
        after=after,
        scratch=scratch,
        moved=12 * 2**20,
    )


def added(parts):
    total = parts[0].astype(F32)
    for part in parts[1:]:
        total = total + part.astype(F32)
    return total.astype(BF16)


class Shards:
    def __init__(self, send, keep, order):
        places, self.shard, self.width = send.shape
        bits = places.bit_length() - 1
        self.shape = (2,) * bits + (self.shard, self.width)
        self.order = list(order)
        self.left = list(range(bits))[::-1]
        self.mine = None
        self.held = [keep.reshape(self.shape)]
        self.coming = flipped(send, "dp", 1).reshape(self.shape)

    def step(self, after=None):
        coming = self.coming
        if after is not None:
            coming, _ = lax.optimization_barrier((coming, after))
        self.held.append(coming)
        if not self.order:
            self.mine = lax.optimization_barrier(added(self.held))
            self.coming = flipped(self.mine, "mod", 1)
            return self.mine
        bit = self.order.pop(0)
        dim = self.left.index(bit)
        away = added([lax.index_in_dim(part, 1, dim, keepdims=False) for part in self.held])
        self.held = [lax.index_in_dim(part, 0, dim, keepdims=False) for part in self.held]
        self.left.remove(bit)
        self.coming = flipped(away, "dp", 2 << bit)
        return away

    def result(self):
        return self.mine.astype(F32) + self.coming.astype(F32)


def reduce_plain(send, keep):
    total = jnp.stack([keep, send], 1)
    total = total.reshape(-1, total.shape[-1]).astype(F32)
    share = lax.psum_scatter(total, "dp", scatter_dimension=0, tiled=True)
    return lax.psum(share.astype(BF16), "mod").astype(F32)


def sum_everywhere(value):
    shards = lax.axis_size("dp")
    if shards & (shards - 1):
        return lax.psum(value, ("mod", "dp"))
    mask = 1
    while mask < shards:
        value = value + flipped(value, "dp", mask)
        mask *= 2
    return value + flipped(value, "mod", 1)


def body(
    layer_rows,
    cotangent,
    row_live,
    partner,
    w_qkv,
    b_qv,
    w_out,
    norm_gains,
    bias_rows,
    w_in,
    b_in,
    w_back,
):
    side = lax.axis_index("mod")
    place = lax.axis_index("dp")
    shards = lax.axis_size("dp")
    groups = partner.shape[1]
    aligned = shards >= 8 and shards & (shards - 1) == 0 and (layer_rows.shape[2] // shards) % 16 == 0
    layout = shards if aligned else 16
    half = groups // 2
    width = layer_rows.shape[2]
    slot_rows = layer_rows.shape[1] // groups
    inner_width = w_in.shape[1]
    slots = (groups, slot_rows, width)
    rows = layer_rows[0].reshape(slots)
    cot = cotangent[0].reshape(slots)
    spot = place if aligned else 0 * place
    scalars = jnp.concatenate(
        [partner[0], jnp.stack([side, spot & 1, spot >> 1]).astype(jnp.int32)]
    )
    cut = half // 2
    sent_a = gather_sent(scalars, rows, half, 0, cut)
    got_a = flipped(sent_a, "mod", 1)
    sent_b = gather_sent(scalars, rows, half, cut, cut, [sent_a])
    got_b = flipped(sent_b, "mod", 1)
    sent_cot = gather_sent(scalars, cot, half, 0, half, [sent_b])
    far_cot = flipped(sent_cot, "mod", 1)

    live = row_live.reshape(2, groups, slot_rows)
    words_live = lax.dynamic_slice_in_dim(live[0], side * half, half, 0)
    region_live = live[1][lax.dynamic_slice_in_dim(partner[0], side * half, half, 0)]
    is_first = side == 0
    seen = jnp.concatenate(
        [
            jnp.where(is_first, words_live, region_live),
            jnp.where(is_first, region_live, words_live),
        ],
        1,
    )[:, None, :]

    heads_weights = (w_qkv, b_qv, w_out, norm_gains, bias_rows)
    first_part = attention_forward(
        scalars, rows, got_a, seen, heads_weights, 0, half, after=[sent_cot]
    )
    joined, mixed, probs, context, normed, root = attention_forward(
        scalars, rows, got_b, seen, heads_weights, cut, half, into=first_part
    )
    feed_weights = (w_in, b_in.reshape(1, inner_width), w_back, norm_gains, bias_rows)
    slope, branch, out_kept, out_far, sums_two, *grads = feed_forward(
        scalars, normed, cot, far_cot, feed_weights, half, layout, groups
    )
    back_weights = (w_in, w_back, norm_gains, bias_rows)
    bits = (layout // 2).bit_length() - 1
    order = list(range(bits))
    other = order[1:] + order[:1]

    def travel(send, keep, steps):
        return Shards(send, keep, steps) if aligned else (send, keep)

    def steps_of(pieces, after):
        return [piece.step(after) for piece in pieces] if aligned else []

    back = [travel(*grads[0:2], order), travel(*grads[2:4], order)]
    sent = steps_of(back[:1], grads[0]) + steps_of(back[1:], grads[0])
    out_back = flipped(out_far, "mod", 1)
    low_attn, sums_one, inner_sum, *grads = feed_backward(
        scalars, branch, slope, normed, root, context, back_weights, layout, groups, after=sent
    )
    inner = [travel(*grads[0:2], order), travel(*grads[2:4], order)]
    outer = travel(*grads[4:6], other)
    sent = steps_of(back, low_attn) + steps_of(inner, low_attn) + steps_of([outer], low_attn)
    attn_kept = (low_attn, mixed, probs, joined)
    attn_weights = (w_out, w_qkv)
    *first_part, sums_qv_a = attention_backward(
        scalars, attn_kept, attn_weights, 0, 2, layout, groups, after=sent
    )
    sent = steps_of(back + [outer], sums_qv_a)
    _, d_kept, d_far, sums_qv_b, *grads = attention_backward(
        scalars, attn_kept, attn_weights, 1, 2, layout, groups, into=first_part, after=sent
    )
    qkv = [
        travel(*grads[0:2], order),
        travel(*grads[2:4], other),
        travel(*grads[4:6], order),
    ]
    d_back = flipped(d_far, "mod", 1)
    pieces = back + inner + [outer] + qkv
    if aligned:
        steps_of(back + inner + [outer], sums_qv_b)
        while any(piece.mine is None for piece in pieces):
            for piece in pieces:
                if piece.mine is None:
                    piece.step()
        done = [piece.result() for piece in pieces]
    else:
        done = [reduce_plain(*piece) for piece in pieces]
    grad_back = jnp.concatenate(done[0:2], 1)
    grad_in = jnp.concatenate(done[2:4], 1)
    grad_out = done[4]
    grad_qkv = jnp.concatenate(done[5:], 1)

    sums_qv = sums_qv_a + sums_qv_b
    small = jnp.concatenate(
        [
            sums_qv[0:2],
            sums_one[0:1],
            sums_two[0:1],
            sums_one[2:3],
            sums_one[1:2],
            sums_two[2:3],
            sums_two[1:2],
            inner_sum[0].reshape(-1, width),
        ],
        0,
    )
    small = sum_everywhere(small)
    shard = width // shards
    rows_small = lax.dynamic_slice_in_dim(small[:8], place * shard, shard, 1)
    inner_shard = inner_width // shards
    grad_b_in = lax.dynamic_slice_in_dim(small[8:].reshape(-1), place * inner_shard, inner_shard)

    out_rows = scatter_home(scalars, out_kept, out_back, half).reshape(1, -1, width)
    grad_rows = scatter_home(scalars, d_kept, d_back, half).reshape(1, -1, width)
    return (
        out_rows,
        grad_rows,
        grad_qkv,
        rows_small[0:2],
        grad_out,
        rows_small[2:4],
        rows_small[4:8],
        grad_in,
        grad_b_in,
        grad_back,
    )


def solution(mesh):
    return jax.shard_map(
        body,
        mesh=mesh,
        in_specs=(
            P("mod", "dp", None),
            P("mod", "dp", None),
            P(None, "dp"),
            P("dp", None),
            P(),
            P(),
            P(),
            P(),
            P(),
            P(),
            P(),
            P(),
        ),
        out_specs=(
            P("mod", "dp", None),
            P("mod", "dp", None),
            P("dp", None),
            P(None, "dp"),
            P("dp", None),
            P(None, "dp"),
            P(None, "dp"),
            P("dp", None),
            P("dp"),
            P("dp", None),
        ),
        check_vma=False,
    )
```

profile of v0, /device:TPU:0, one launch (start us, length us, event | category | flops | bytes accessed | tf_op | source)
XLA Modules:
  0.0 319.5 jit_solution(15388018786166938267)
XLA Ops:
  3.9 3.0 collective-permute-start.1
  8.1 1.7 gather_sent.5.refs_9_
  9.8 2.0 collective-permute-start.2
  13.4 3.5 %collective-permute-done.1.refs_2_ = bf16[4,64,768]{2,1,0:T(8,128)(2,1)S(1)} collective-permute-done((bf16[4,64,768]{2,1,0:T(8,128)(2,1)S(1)}, bf16[4,64,768]{2,1,0:T(8,128)(2,1)S(1)}, u32[]{:S(2)}, u32[]{:S(2)}) %collective-permute-start.1) | collective-permute-done | bytes 393248 | tf_op jit(solution)/shard_map/ppermute | solution.py:25
  17.6 10.1 %attention_forward.2 = (bf16[1024,768]{1,0:T(8,128)(2,1)}, bf16[1024,2304]{1,0:T(8,128)(2,1)}, bf16[8,6,256,128]{3,2,1,0:T(8,128)(2,1)}, bf16[1024,768]{1,0:T(8,...) custom-call(s32[19]{0:T(128)} %copy-done.5, bf16[16,64,768]{2,1,0:T(8,128)(2,1)} %bitcast.264, ...), custom_call_target="tpu_custom_call" | custom-call | flops 3019898880 | bytes 12582912 | tf_op jit(solution)/shard_map/attention_forward/pallas_call | solution.py:58
  28.5 10.2 %attention_forward.3 = (bf16[1024,768]{1,0:T(8,128)(2,1)}, bf16[1024,2304]{1,0:T(8,128)(2,1)}, bf16[8,6,256,128]{3,2,1,0:T(8,128)(2,1)}, bf16[1024,768]{1,0:T(8,...) custom-call(s32[19]{0:T(128)} %copy-done.5, ...), custom_call_target="tpu_custom_call", output_to_operand_aliasing={{0}: (10, {}), {1}: (11, {}), {2}: (12, {}), {3}: (13, {}),... | custom-call | flops 3019898880 | bytes 12582912 | tf_op jit(solution)/shard_map/attention_forward/pallas_call | solution.py:58
  38.7 2.6 collective-permute-done.2.refs_3_
  42.2 29.5 %feed_forward.1 = (bf16[1024,3072]{1,0:T(8,128)(2,1)}, bf16[1024,768]{1,0:T(8,128)(2,1)}, bf16[8,64,768]{2,1,0:T(8,128)(2,1)}, bf16[8,64,768]{2,1,0:T(8,128)(2,1...) custom-call(s32[19]{0:T(128)} %copy-done.5, ...), custom_call_target="tpu_custom_call" | custom-call | flops 14495514624 | bytes 29360128 | tf_op jit(solution)/shard_map/feed_forward/pallas_call | solution.py:58
  72.3 1.7 collective-permute-start.3
  76.8 15.2 %collective-permute-done.3.refs_1_ = bf16[8,64,768]{2,1,0:T(8,128)(2,1)S(1)} collective-permute-done((bf16[8,64,768]{2,1,0:T(8,128)(2,1)}, bf16[8,64,768]{2,1,0:T(8,128)(2,1)S(1)}, u32[]{:S(2)}, u32[]{:S(2)}) %collective-permute-start.3) | collective-permute-done | bytes 786464 | tf_op jit(solution)/shard_map/ppermute | solution.py:25
  92.1 3.9 %scatter_home.2 = bf16[16,64,768]{2,1,0:T(8,128)(2,1)} custom-call(s32[19]{0:T(128)S(1)} %copy-done.6, bf16[8,64,768]{2,1,0:T(8,128)(2,1)S(1)} %copy-done.4, bf16[8,64,768]{2,1,0:T(8,128)(2,1)S(1)} %collective-permute-done.3.refs_1_), custom_call_target="tpu_custom_call" | custom-call | flops 1000000 | bytes 1048576 | tf_op jit(solution)/shard_map/scatter_home/pallas_call | solution.py:58
  97.4 2.6 fusion
  100.0 1.8 collective-permute-start.6
  102.0 27.4 %feed_backward.1 = (bf16[1024,768]{1,0:T(8,128)(2,1)}, f32[8,768]{1,0:T(8,128)}, f32[8,3072]{1,0:T(8,128)}, bf16[8,48,1536]{2,1,0:T(8,128)(2,1)}, bf16[8,48,1536...) custom-call(s32[19]{0:T(128)} %copy-done.5, ...), custom_call_target="tpu_custom_call" | custom-call | flops 14495514624 | bytes 27262976 | tf_op jit(solution)/shard_map/feed_backward/pallas_call | solution.py:58
  136.9 1.9 collective-permute-start.13
  141.4 1.7 collective-permute-start.12
  143.2 2.0 fusion.2.refs_7_
  145.2 1.5 collective-permute-start.38
  148.7 16.6 %attention_backward.2 = (bf16[1024,2304]{1,0:T(8,128)(2,1)}, bf16[8,64,768]{2,1,0:T(8,128)(2,1)}, bf16[8,64,768]{2,1,0:T(8,128)(2,1)}, f32[8,768]{1,0:T(8,128)}) custom-call(s32[19]{0:T(128)} %copy-done.5, bf16[1024,768]{1,0:T(8,128)(2,1)} %get-tuple-element.87.refs_0_, bf16[1024,2304]{1,0:T(8,128)(2,1)} %get-tuple-element.88.refs_1_, ...), custom_call_target="tpu_custom_call" | custom-call | flops 6039797760 | bytes 12582912 | tf_op jit(solution)/shard_map/attention_backward/pallas_call | solution.py:58
  166.7 1.8 fusion.25.refs_9_
  168.5 1.6 fusion.24.refs_10_
  170.2 1.7 fusion.23.refs_11_
  171.9 23.8 %attention_backward.3 = (bf16[256,2304]{1,0:T(8,128)(2,1)}, bf16[8,64,768]{2,1,0:T(8,128)(2,1)}, bf16[8,64,768]{2,1,0:T(8,128)(2,1)}, f32[8,768]{1,0:T(8,128)}, ...) custom-call(s32[19]{0:T(128)} %copy-done.5, ...), custom_call_target="tpu_custom_call", output_to_operand_aliasing={{1}: (8, {}), {2}: (9, {})} | custom-call | flops 6039797760 | bytes 12582912 | tf_op jit(solution)/shard_map/attention_backward/pallas_call | solution.py:58
  199.6 2.6 collective-permute-start.35
  205.6 10.3 %collective-permute-done.31 = f32[12,768]{1,0:T(8,128)S(1)} collective-permute-done((f32[12,768]{1,0:T(8,128)S(1)}, f32[12,768]{1,0:T(8,128)S(1)}, u32[]{:S(2)}, u32[]{:S(2)}) %collective-permute-start.31) | collective-permute-done | bytes 36896 | tf_op jit(solution)/shard_map/ppermute | solution.py:25
  217.3 2.9 collective-permute-done.32
  220.2 2.8 collective-permute-start.46
  223.0 1.7 fusion.13
  224.8 3.6 %collective-permute-done.46 = bf16[192,384]{1,0:T(8,128)(2,1)S(1)} collective-permute-done((bf16[192,384]{1,0:T(8,128)(2,1)S(1)}, bf16[192,384]{1,0:T(8,128)(2,1)S(1)}, u32[]{:S(2)}, u32[]{:S(2)}) %collective-permute-start.46) | collective-permute-done | bytes 147488 | tf_op jit(solution)/shard_map/ppermute | solution.py:25
  230.3 3.3 %collective-permute-done.33 = f32[12,768]{1,0:T(8,128)S(1)} collective-permute-done((f32[12,768]{1,0:T(8,128)S(1)}, f32[12,768]{1,0:T(8,128)S(1)}, u32[]{:S(2)}, u32[]{:S(2)}) %collective-permute-start.33) | collective-permute-done | bytes 36896 | tf_op jit(solution)/shard_map/ppermute | solution.py:25
  233.6 1.6 collective-permute-start.34
  236.1 1.6 collective-permute-done.34
  240.1 1.9 collective-permute-done.36
  244.6 2.6 collective-permute-done.49
  248.8 2.8 collective-permute-done.37
  253.7 3.0 collective-permute-done.47
  268.5 9.1 %collective-permute-done.14.refs_1_ = bf16[8,64,768]{2,1,0:T(8,128)(2,1)S(1)} collective-permute-done((bf16[8,64,768]{2,1,0:T(8,128)(2,1)S(1)}, bf16[8,64,768]{2,1,0:T(8,128)(2,1)S(1)}, u32[]{:S(2)}, u32[]{:S(2)}) %collective-permute-start.14) | collective-permute-done | bytes 786464 | tf_op jit(solution)/shard_map/ppermute | solution.py:25
  278.1 3.9 %scatter_home.3 = bf16[16,64,768]{2,1,0:T(8,128)(2,1)} custom-call(s32[19]{0:T(128)S(1)} %copy-done.7, bf16[8,64,768]{2,1,0:T(8,128)(2,1)S(1)} %copy-done.1, bf16[8,64,768]{2,1,0:T(8,128)(2,1)S(1)} %collective-permute-done.14.refs_1_), custom_call_target="tpu_custom_call" | custom-call | flops 1000000 | bytes 1048576 | tf_op jit(solution)/shard_map/scatter_home/pallas_call | solution.py:58
  285.1 2.1 collective-permute-start.40
  289.4 2.5 collective-permute-start.22
  292.1 5.9 %collective-permute-done.44 = bf16[48,1536]{1,0:T(8,128)(2,1)S(1)} collective-permute-done((bf16[48,1536]{1,0:T(8,128)(2,1)S(1)}, bf16[48,1536]{1,0:T(8,128)(2,1)S(1)}, u32[]{:S(2)}, u32[]{:S(2)}) %collective-permute-start.44) | collective-permute-done | bytes 147488 | tf_op jit(solution)/shard_map/ppermute | solution.py:25
  299.0 1.6 collective-permute-start.45
  300.6 2.1 collective-permute-done.40
  303.6 1.6 collective-permute-start.41
  306.3 1.6 collective-permute-start.23
  307.9 3.0 collective-permute-start.28
  312.5 1.6 collective-permute-start.24
  316.9 1.6 collective-permute-done.29
  (236 shorter events, 72.9 us)
Async XLA Ops:
  3.9 12.9 %collective-permute-start.1 = (bf16[4,64,768]{2,1,0:T(8,128)(2,1)S(1)}, bf16[4,64,768]{2,1,0:T(8,128)(2,1)S(1)}, u32[]{:S(2)}, u32[]{:S(2)}) collective-permute-start(bf16[4,64,768]{2,1,0:T(8,128)(2,1)S(1)} %gather_sent.3.refs_1_), channel_id=1, source_target_pairs={{0,16},{16,0},{1,17},{17,1},{2,18},{18,2},{3,19},{19,3},{4,20},{20... | collective-permute-start | bytes 1179656 | tf_op jit(solution)/shard_map/ppermute | solution.py:25
  8.0 19.7 %collective-permute-start = (bf16[4,64,768]{2,1,0:T(8,128)(2,1)S(1)}, bf16[4,64,768]{2,1,0:T(8,128)(2,1)S(1)}, u32[]{:S(2)}, u32[]{:S(2)}) collective-permute-start(bf16[4,64,768]{2,1,0:T(8,128)(2,1)S(1)} %gather_sent.4.refs_1_), channel_id=1, source_target_pairs={{0,16},{16,0},{1,17},{17,1},{2,18},{18,2},{3,19},{19,3},{4,20},{20... | collective-permute-start | bytes 1179656 | tf_op jit(solution)/shard_map/ppermute | solution.py:25
  9.8 31.5 %collective-permute-start.2 = (bf16[8,64,768]{2,1,0:T(8,128)(2,1)S(1)}, bf16[8,64,768]{2,1,0:T(8,128)(2,1)S(1)}, u32[]{:S(2)}, u32[]{:S(2)}) collective-permute-start(bf16[8,64,768]{2,1,0:T(8,128)(2,1)S(1)} %gather_sent.5.refs_9_), channel_id=1, source_target_pairs={{0,16},{16,0},{1,17},{17,1},{2,18},{18,2},{3,19},{19,3},{4,20},{20... | collective-permute-start | bytes 2359304 | tf_op jit(solution)/shard_map/ppermute | solution.py:25
  71.8 24.2 %collective-permute-start.5 = (bf16[8,192,384]{2,1,0:T(8,128)(2,1)}, bf16[8,192,384]{2,1,0:T(8,128)(2,1)}, u32[]{:S(2)}, u32[]{:S(2)}) collective-permute-start(bf16[8,192,384]{2,1,0:T(8,128)(2,1)} %get-tuple-element.85), channel_id=1, source_target_pairs={{0,1},{1,0},{2,3},{3,2},{4,5},{5,4},{6,7},{7,6},{8,9},{9,8},{10,11... | collective-permute-start | bytes 3538952 | tf_op jit(solution)/shard_map/ppermute | solution.py:25
  71.8 25.4 %collective-permute-start.4 = (bf16[8,192,384]{2,1,0:T(8,128)(2,1)}, bf16[8,192,384]{2,1,0:T(8,128)(2,1)}, u32[]{:S(2)}, u32[]{:S(2)}) collective-permute-start(bf16[8,192,384]{2,1,0:T(8,128)(2,1)} %get-tuple-element.82), channel_id=1, source_target_pairs={{0,1},{1,0},{2,3},{3,2},{4,5},{5,4},{6,7},{7,6},{8,9},{9,8},{10,11... | collective-permute-start | bytes 3538952 | tf_op jit(solution)/shard_map/ppermute | solution.py:25
  72.3 19.7 %collective-permute-start.3 = (bf16[8,64,768]{2,1,0:T(8,128)(2,1)}, bf16[8,64,768]{2,1,0:T(8,128)(2,1)S(1)}, u32[]{:S(2)}, u32[]{:S(2)}) collective-permute-start(bf16[8,64,768]{2,1,0:T(8,128)(2,1)} %get-tuple-element.76), channel_id=1, source_target_pairs={{0,16},{16,0},{1,17},{17,1},{2,18},{18,2},{3,19},{19,3},{4,20},{20... | collective-permute-start | bytes 2359304 | tf_op jit(solution)/shard_map/ppermute | solution.py:25
  100.0 38.8 %collective-permute-start.6 = (bf16[2,2,192,384]{3,2,1,0:T(8,128)(2,1)}, bf16[2,2,192,384]{3,2,1,0:T(8,128)(2,1)}, u32[]{:S(2)}, u32[]{:S(2)}) collective-permute-start(bf16[2,2,192,384]{3,2,1,0:T(8,128)(2,1)} %get-tuple-element.138.refs_9_), channel_id=1, source_target_pairs={{0,2},{1,3},{2,0},{3,1},{4,6},{5,7},{6,4},{7,5},{8,10},{9,11},{10,... | collective-permute-start | bytes 1769480 | tf_op jit(solution)/shard_map/ppermute | solution.py:25
  101.8 38.6 %collective-permute-start.7 = (bf16[2,2,192,384]{3,2,1,0:T(8,128)(2,1)}, bf16[2,2,192,384]{3,2,1,0:T(8,128)(2,1)}, u32[]{:S(2)}, u32[]{:S(2)}) collective-permute-start(bf16[2,2,192,384]{3,2,1,0:T(8,128)(2,1)} %get-tuple-element.139.refs_10_), channel_id=1, source_target_pairs={{0,2},{1,3},{2,0},{3,1},{4,6},{5,7},{6,4},{7,5},{8,10},{9,11},{10,... | collective-permute-start | bytes 1769480 | tf_op jit(solution)/shard_map/ppermute | solution.py:25
  130.9 4.8 %collective-permute-start.10 = (bf16[8,48,768]{2,1,0:T(8,128)(2,1)}, bf16[8,48,768]{2,1,0:T(8,128)(2,1)}, u32[]{:S(2)}, u32[]{:S(2)}) collective-permute-start(bf16[8,48,768]{2,1,0:T(8,128)(2,1)} %get-tuple-element.100), channel_id=1, source_target_pairs={{0,1},{1,0},{2,3},{3,2},{4,5},{5,4},{6,7},{7,6},{8,9},{9,8},{10,11... | collective-permute-start | bytes 1769480 | tf_op jit(solution)/shard_map/ppermute | solution.py:25
  131.0 12.1 %collective-permute-start.8 = (bf16[8,48,1536]{2,1,0:T(8,128)(2,1)}, bf16[8,48,1536]{2,1,0:T(8,128)(2,1)}, u32[]{:S(2)}, u32[]{:S(2)}) collective-permute-start(bf16[8,48,1536]{2,1,0:T(8,128)(2,1)} %get-tuple-element.94), channel_id=1, source_target_pairs={{0,1},{1,0},{2,3},{3,2},{4,5},{5,4},{6,7},{7,6},{8,9},{9,8},{10,11... | collective-permute-start | bytes 3538952 | tf_op jit(solution)/shard_map/ppermute | solution.py:25
  135.7 11.0 %collective-permute-start.9 = (bf16[8,48,1536]{2,1,0:T(8,128)(2,1)}, bf16[8,48,1536]{2,1,0:T(8,128)(2,1)S(1)}, u32[]{:S(2)}, u32[]{:S(2)}) collective-permute-start(bf16[8,48,1536]{2,1,0:T(8,128)(2,1)} %get-tuple-element.97), channel_id=1, source_target_pairs={{0,1},{1,0},{2,3},{3,2},{4,5},{5,4},{6,7},{7,6},{8,9},{9,8},{10,11... | collective-permute-start | bytes 3538952 | tf_op jit(solution)/shard_map/ppermute | solution.py:25
  136.9 28.4 %collective-permute-start.13 = (bf16[2,2,48,768]{3,2,1,0:T(8,128)(2,1)S(1)}, bf16[2,2,48,768]{3,2,1,0:T(8,128)(2,1)S(1)}, u32[]{:S(2)}, u32[]{:S(2)}) collective-permute-start(bf16[2,2,48,768]{3,2,1,0:T(8,128)(2,1)S(1)} %fusion.6.refs_9_), channel_id=1, source_target_pairs={{0,4},{1,5},{2,6},{3,7},{4,0},{5,1},{6,2},{7,3},{8,12},{9,13},{10,... | collective-permute-start | bytes 884744 | tf_op jit(solution)/shard_map/ppermute | solution.py:25
  139.9 26.8 %collective-permute-start.11 = (bf16[2,192,384]{2,1,0:T(8,128)(2,1)S(1)}, bf16[2,192,384]{2,1,0:T(8,128)(2,1)S(1)}, u32[]{:S(2)}, u32[]{:S(2)}) collective-permute-start(bf16[2,192,384]{2,1,0:T(8,128)(2,1)S(1)} %fusion.4.refs_5_), channel_id=1, source_target_pairs={{0,4},{1,5},{2,6},{3,7},{4,0},{5,1},{6,2},{7,3},{8,12},{9,13},{10,... | collective-permute-start | bytes 884744 | tf_op jit(solution)/shard_map/ppermute | solution.py:25
  141.4 23.9 %collective-permute-start.12 = (bf16[2,192,384]{2,1,0:T(8,128)(2,1)S(1)}, bf16[2,192,384]{2,1,0:T(8,128)(2,1)S(1)}, u32[]{:S(2)}, u32[]{:S(2)}) collective-permute-start(bf16[2,192,384]{2,1,0:T(8,128)(2,1)S(1)} %fusion.5.refs_6_), channel_id=1, source_target_pairs={{0,4},{1,5},{2,6},{3,7},{4,0},{5,1},{6,2},{7,3},{8,12},{9,13},{10,... | collective-permute-start | bytes 884744 | tf_op jit(solution)/shard_map/ppermute | solution.py:25
  145.2 117.1 %collective-permute-start.38 = (bf16[2,2,48,1536]{3,2,1,0:T(8,128)(2,1)}, bf16[2,2,48,1536]{3,2,1,0:T(8,128)(2,1)}, u32[]{:S(2)}, u32[]{:S(2)}) collective-permute-start(bf16[2,2,48,1536]{3,2,1,0:T(8,128)(2,1)} %fusion.2.refs_7_), channel_id=1, source_target_pairs={{0,2},{1,3},{2,0},{3,1},{4,6},{5,7},{6,4},{7,5},{8,10},{9,11},{10,... | collective-permute-start | bytes 1769480 | tf_op jit(solution)/shard_map/ppermute | solution.py:25
  197.7 4.8 %collective-permute-start.30 = (f32[12,768]{1,0:T(8,128)}, f32[12,768]{1,0:T(8,128)S(1)}, u32[]{:S(2)}, u32[]{:S(2)}) collective-permute-start(f32[12,768]{1,0:T(8,128)} %concatenate.21), channel_id=1, source_target_pairs={{0,1},{1,0},{2,3},{3,2},{4,5},{5,4},{6,7},{7,6},{8,9},{9,8},{10,11... | collective-permute-start | bytes 110600 | tf_op jit(solution)/shard_map/ppermute | solution.py:25
  199.0 58.6 %collective-permute-start.42 = (bf16[2,2,48,1536]{3,2,1,0:T(8,128)(2,1)}, bf16[2,2,48,1536]{3,2,1,0:T(8,128)(2,1)}, u32[]{:S(2)}, u32[]{:S(2)}) collective-permute-start(bf16[2,2,48,1536]{3,2,1,0:T(8,128)(2,1)} %fusion.3.refs_8_), channel_id=1, source_target_pairs={{0,2},{1,3},{2,0},{3,1},{4,6},{5,7},{6,4},{7,5},{8,10},{9,11},{10,... | collective-permute-start | bytes 1769480 | tf_op jit(solution)/shard_map/ppermute | solution.py:25
  199.6 30.5 %collective-permute-start.35 = (bf16[2,48,768]{2,1,0:T(8,128)(2,1)}, bf16[2,48,768]{2,1,0:T(8,128)(2,1)S(1)}, u32[]{:S(2)}, u32[]{:S(2)}) collective-permute-start(bf16[2,48,768]{2,1,0:T(8,128)(2,1)} %fusion.23.refs_11_), channel_id=1, source_target_pairs={{0,8},{1,9},{2,10},{3,11},{4,12},{5,13},{6,14},{7,15},{8,0},{9,1},... | collective-permute-start | bytes 442376 | tf_op jit(solution)/shard_map/ppermute | solution.py:25
  202.2 20.7 %collective-permute-start.48 = (bf16[192,384]{1,0:T(8,128)(2,1)}, bf16[192,384]{1,0:T(8,128)(2,1)S(1)}, u32[]{:S(2)}, u32[]{:S(2)}) collective-permute-start(bf16[192,384]{1,0:T(8,128)(2,1)} %fusion.24.refs_10_), channel_id=1, source_target_pairs={{0,8},{1,9},{2,10},{3,11},{4,12},{5,13},{6,14},{7,15},{8,0},{9,1},... | collective-permute-start | bytes 442376 | tf_op jit(solution)/shard_map/ppermute | solution.py:25
  203.4 12.6 %collective-permute-start.31 = (f32[12,768]{1,0:T(8,128)S(1)}, f32[12,768]{1,0:T(8,128)S(1)}, u32[]{:S(2)}, u32[]{:S(2)}) collective-permute-start(f32[12,768]{1,0:T(8,128)S(1)} %add.451), channel_id=1, source_target_pairs={{0,2},{1,3},{2,0},{3,1},{4,6},{5,7},{6,4},{7,5},{8,10},{9,11},{10,... | collective-permute-start | bytes 110600 | tf_op jit(solution)/shard_map/ppermute | solution.py:25
  220.2 8.2 %collective-permute-start.46 = (bf16[192,384]{1,0:T(8,128)(2,1)S(1)}, bf16[192,384]{1,0:T(8,128)(2,1)S(1)}, u32[]{:S(2)}, u32[]{:S(2)}) collective-permute-start(bf16[192,384]{1,0:T(8,128)(2,1)S(1)} %copy-done.25), channel_id=1, source_target_pairs={{0,8},{1,9},{2,10},{3,11},{4,12},{5,13},{6,14},{7,15},{8,0},{9,1},... | collective-permute-start | bytes 442376 | tf_op jit(solution)/shard_map/ppermute | solution.py:25
  222.9 37.3 %collective-permute-start.15 = (bf16[8,48,768]{2,1,0:T(8,128)(2,1)}, bf16[8,48,768]{2,1,0:T(8,128)(2,1)}, u32[]{:S(2)}, u32[]{:S(2)}) collective-permute-start(bf16[8,48,768]{2,1,0:T(8,128)(2,1)} %get-tuple-element.112), channel_id=1, source_target_pairs={{0,1},{1,0},{2,3},{3,2},{4,5},{5,4},{6,7},{7,6},{8,9},{9,8},{10,11... | collective-permute-start | bytes 1769480 | tf_op jit(solution)/shard_map/ppermute | solution.py:25
  228.4 5.2 %collective-permute-start.33 = (f32[12,768]{1,0:T(8,128)S(1)}, f32[12,768]{1,0:T(8,128)S(1)}, u32[]{:S(2)}, u32[]{:S(2)}) collective-permute-start(f32[12,768]{1,0:T(8,128)S(1)} %add.453), channel_id=1, source_target_pairs={{0,8},{1,9},{2,10},{3,11},{4,12},{5,13},{6,14},{7,15},{8,0},{9,1},... | collective-permute-start | bytes 110600 | tf_op jit(solution)/shard_map/ppermute | solution.py:25
  230.2 35.4 %collective-permute-start.20 = (bf16[8,48,768]{2,1,0:T(8,128)(2,1)}, bf16[8,48,768]{2,1,0:T(8,128)(2,1)}, u32[]{:S(2)}, u32[]{:S(2)}) collective-permute-start(bf16[8,48,768]{2,1,0:T(8,128)(2,1)} %get-tuple-element.114), channel_id=1, source_target_pairs={{0,1},{1,0},{2,3},{3,2},{4,5},{5,4},{6,7},{7,6},{8,9},{9,8},{10,11... | collective-permute-start | bytes 1769480 | tf_op jit(solution)/shard_map/ppermute | solution.py:25
  237.7 4.4 %collective-permute-start.36 = (bf16[48,768]{1,0:T(8,128)(2,1)S(1)}, bf16[48,768]{1,0:T(8,128)(2,1)S(1)}, u32[]{:S(2)}, u32[]{:S(2)}) collective-permute-start(bf16[48,768]{1,0:T(8,128)(2,1)S(1)} %fusion.28), channel_id=1, source_target_pairs={{0,2},{1,3},{2,0},{3,1},{4,6},{5,7},{6,4},{7,5},{8,10},{9,11},{10,... | collective-permute-start | bytes 221192 | tf_op jit(solution)/shard_map/ppermute | solution.py:25
  242.1 5.1 %collective-permute-start.49 = (bf16[192,384]{1,0:T(8,128)(2,1)S(1)}, bf16[192,384]{1,0:T(8,128)(2,1)S(1)}, u32[]{:S(2)}, u32[]{:S(2)}) collective-permute-start(bf16[192,384]{1,0:T(8,128)(2,1)S(1)} %copy-done.24), channel_id=1, source_target_pairs={{0,16},{16,0},{1,17},{17,1},{2,18},{18,2},{3,19},{19,3},{4,20},{20... | collective-permute-start | bytes 442376 | tf_op jit(solution)/shard_map/ppermute | solution.py:25
  247.2 4.4 %collective-permute-start.37 = (bf16[48,768]{1,0:T(8,128)(2,1)S(1)}, bf16[48,768]{1,0:T(8,128)(2,1)S(1)}, u32[]{:S(2)}, u32[]{:S(2)}) collective-permute-start(bf16[48,768]{1,0:T(8,128)(2,1)S(1)} %fusion.30), channel_id=1, source_target_pairs={{0,16},{16,0},{1,17},{17,1},{2,18},{18,2},{3,19},{19,3},{4,20},{20... | collective-permute-start | bytes 221192 | tf_op jit(solution)/shard_map/ppermute | solution.py:25
  251.6 5.1 %collective-permute-start.47 = (bf16[192,384]{1,0:T(8,128)(2,1)S(1)}, bf16[192,384]{1,0:T(8,128)(2,1)S(1)}, u32[]{:S(2)}, u32[]{:S(2)}) collective-permute-start(bf16[192,384]{1,0:T(8,128)(2,1)S(1)} %fusion.15), channel_id=1, source_target_pairs={{0,16},{16,0},{1,17},{17,1},{2,18},{18,2},{3,19},{19,3},{4,20},{20... | collective-permute-start | bytes 442376 | tf_op jit(solution)/shard_map/ppermute | solution.py:25
  256.7 10.5 %collective-permute-start.25 = (bf16[8,48,768]{2,1,0:T(8,128)(2,1)}, bf16[8,48,768]{2,1,0:T(8,128)(2,1)S(1)}, u32[]{:S(2)}, u32[]{:S(2)}) collective-permute-start(bf16[8,48,768]{2,1,0:T(8,128)(2,1)} %get-tuple-element.116), channel_id=1, source_target_pairs={{0,1},{1,0},{2,3},{3,2},{4,5},{5,4},{6,7},{7,6},{8,9},{9,8},{10,11... | collective-permute-start | bytes 1769480 | tf_op jit(solution)/shard_map/ppermute | solution.py:25
  257.6 20.0 %collective-permute-start.14 = (bf16[8,64,768]{2,1,0:T(8,128)(2,1)S(1)}, bf16[8,64,768]{2,1,0:T(8,128)(2,1)S(1)}, u32[]{:S(2)}, u32[]{:S(2)}) collective-permute-start(bf16[8,64,768]{2,1,0:T(8,128)(2,1)S(1)} %copy-done.18), channel_id=1, source_target_pairs={{0,16},{16,0},{1,17},{17,1},{2,18},{18,2},{3,19},{19,3},{4,20},{20... | collective-permute-start | bytes 2359304 | tf_op jit(solution)/shard_map/ppermute | solution.py:25
  262.3 19.7 %collective-permute-start.43 = (bf16[2,48,1536]{2,1,0:T(8,128)(2,1)S(1)}, bf16[2,48,1536]{2,1,0:T(8,128)(2,1)S(1)}, u32[]{:S(2)}, u32[]{:S(2)}) collective-permute-start(bf16[2,48,1536]{2,1,0:T(8,128)(2,1)S(1)} %fusion.11), channel_id=1, source_target_pairs={{0,4},{1,5},{2,6},{3,7},{4,0},{5,1},{6,2},{7,3},{8,12},{9,13},{10,... | collective-permute-start | bytes 884744 | tf_op jit(solution)/shard_map/ppermute | solution.py:25
  264.6 19.5 %collective-permute-start.39 = (bf16[2,48,1536]{2,1,0:T(8,128)(2,1)S(1)}, bf16[2,48,1536]{2,1,0:T(8,128)(2,1)S(1)}, u32[]{:S(2)}, u32[]{:S(2)}) collective-permute-start(bf16[2,48,1536]{2,1,0:T(8,128)(2,1)S(1)} %fusion.10), channel_id=1, source_target_pairs={{0,4},{1,5},{2,6},{3,7},{4,0},{5,1},{6,2},{7,3},{8,12},{9,13},{10,... | collective-permute-start | bytes 884744 | tf_op jit(solution)/shard_map/ppermute | solution.py:25
  265.6 21.6 %collective-permute-start.16 = (bf16[2,2,48,768]{3,2,1,0:T(8,128)(2,1)S(1)}, bf16[2,2,48,768]{3,2,1,0:T(8,128)(2,1)S(1)}, u32[]{:S(2)}, u32[]{:S(2)}) collective-permute-start(bf16[2,2,48,768]{3,2,1,0:T(8,128)(2,1)S(1)} %fusion.7), channel_id=1, source_target_pairs={{0,2},{1,3},{2,0},{3,1},{4,6},{5,7},{6,4},{7,5},{8,10},{9,11},{10,... | collective-permute-start | bytes 884744 | tf_op jit(solution)/shard_map/ppermute | solution.py:25
  267.2 21.2 %collective-permute-start.21 = (bf16[2,2,48,768]{3,2,1,0:T(8,128)(2,1)S(1)}, bf16[2,2,48,768]{3,2,1,0:T(8,128)(2,1)S(1)}, u32[]{:S(2)}, u32[]{:S(2)}) collective-permute-start(bf16[2,2,48,768]{3,2,1,0:T(8,128)(2,1)S(1)} %fusion.8), channel_id=1, source_target_pairs={{0,4},{1,5},{2,6},{3,7},{4,0},{5,1},{6,2},{7,3},{8,12},{9,13},{10,... | collective-permute-start | bytes 884744 | tf_op jit(solution)/shard_map/ppermute | solution.py:25
  277.6 14.4 %collective-permute-start.26 = (bf16[2,2,48,768]{3,2,1,0:T(8,128)(2,1)S(1)}, bf16[2,2,48,768]{3,2,1,0:T(8,128)(2,1)S(1)}, u32[]{:S(2)}, u32[]{:S(2)}) collective-permute-start(bf16[2,2,48,768]{3,2,1,0:T(8,128)(2,1)S(1)} %fusion.9), channel_id=1, source_target_pairs={{0,2},{1,3},{2,0},{3,1},{4,6},{5,7},{6,4},{7,5},{8,10},{9,11},{10,... | collective-permute-start | bytes 884744 | tf_op jit(solution)/shard_map/ppermute | solution.py:25
  283.1 14.9 %collective-permute-start.44 = (bf16[48,1536]{1,0:T(8,128)(2,1)S(1)}, bf16[48,1536]{1,0:T(8,128)(2,1)S(1)}, u32[]{:S(2)}, u32[]{:S(2)}) collective-permute-start(bf16[48,1536]{1,0:T(8,128)(2,1)S(1)} %fusion.16), channel_id=1, source_target_pairs={{0,8},{1,9},{2,10},{3,11},{4,12},{5,13},{6,14},{7,15},{8,0},{9,1},... | collective-permute-start | bytes 442376 | tf_op jit(solution)/shard_map/ppermute | solution.py:25
  285.1 17.5 %collective-permute-start.40 = (bf16[48,1536]{1,0:T(8,128)(2,1)S(1)}, bf16[48,1536]{1,0:T(8,128)(2,1)S(1)}, u32[]{:S(2)}, u32[]{:S(2)}) collective-permute-start(bf16[48,1536]{1,0:T(8,128)(2,1)S(1)} %fusion.19), channel_id=1, source_target_pairs={{0,8},{1,9},{2,10},{3,11},{4,12},{5,13},{6,14},{7,15},{8,0},{9,1},... | collective-permute-start | bytes 442376 | tf_op jit(solution)/shard_map/ppermute | solution.py:25
  287.2 18.0 %collective-permute-start.17 = (bf16[2,48,768]{2,1,0:T(8,128)(2,1)S(1)}, bf16[2,48,768]{2,1,0:T(8,128)(2,1)S(1)}, u32[]{:S(2)}, u32[]{:S(2)}) collective-permute-start(bf16[2,48,768]{2,1,0:T(8,128)(2,1)S(1)} %fusion.26), channel_id=1, source_target_pairs={{0,4},{1,5},{2,6},{3,7},{4,0},{5,1},{6,2},{7,3},{8,12},{9,13},{10,... | collective-permute-start | bytes 442376 | tf_op jit(solution)/shard_map/ppermute | solution.py:25
  289.4 15.9 %collective-permute-start.22 = (bf16[2,48,768]{2,1,0:T(8,128)(2,1)S(1)}, bf16[2,48,768]{2,1,0:T(8,128)(2,1)S(1)}, u32[]{:S(2)}, u32[]{:S(2)}) collective-permute-start(bf16[2,48,768]{2,1,0:T(8,128)(2,1)S(1)} %fusion.22), channel_id=1, source_target_pairs={{0,8},{1,9},{2,10},{3,11},{4,12},{5,13},{6,14},{7,15},{8,0},{9,1},... | collective-permute-start | bytes 442376 | tf_op jit(solution)/shard_map/ppermute | solution.py:25
  292.0 15.9 %collective-permute-start.27 = (bf16[2,48,768]{2,1,0:T(8,128)(2,1)S(1)}, bf16[2,48,768]{2,1,0:T(8,128)(2,1)S(1)}, u32[]{:S(2)}, u32[]{:S(2)}) collective-permute-start(bf16[2,48,768]{2,1,0:T(8,128)(2,1)S(1)} %fusion.27), channel_id=1, source_target_pairs={{0,4},{1,5},{2,6},{3,7},{4,0},{5,1},{6,2},{7,3},{8,12},{9,13},{10,... | collective-permute-start | bytes 442376 | tf_op jit(solution)/shard_map/ppermute | solution.py:25
  299.0 16.3 %collective-permute-start.45 = (bf16[48,1536]{1,0:T(8,128)(2,1)S(1)}, bf16[48,1536]{1,0:T(8,128)(2,1)S(1)}, u32[]{:S(2)}, u32[]{:S(2)}) collective-permute-start(bf16[48,1536]{1,0:T(8,128)(2,1)S(1)} %fusion.18), channel_id=1, source_target_pairs={{0,16},{16,0},{1,17},{17,1},{2,18},{18,2},{3,19},{19,3},{4,20},{20... | collective-permute-start | bytes 442376 | tf_op jit(solution)/shard_map/ppermute | solution.py:25
  303.6 11.8 %collective-permute-start.41 = (bf16[48,1536]{1,0:T(8,128)(2,1)S(1)}, bf16[48,1536]{1,0:T(8,128)(2,1)S(1)}, u32[]{:S(2)}, u32[]{:S(2)}) collective-permute-start(bf16[48,1536]{1,0:T(8,128)(2,1)S(1)} %fusion.21), channel_id=1, source_target_pairs={{0,16},{16,0},{1,17},{17,1},{2,18},{18,2},{3,19},{19,3},{4,20},{20... | collective-permute-start | bytes 442376 | tf_op jit(solution)/shard_map/ppermute | solution.py:25
  305.2 5.6 %collective-permute-start.18 = (bf16[48,768]{1,0:T(8,128)(2,1)S(1)}, bf16[48,768]{1,0:T(8,128)(2,1)S(1)}, u32[]{:S(2)}, u32[]{:S(2)}) collective-permute-start(bf16[48,768]{1,0:T(8,128)(2,1)S(1)} %fusion.37), channel_id=1, source_target_pairs={{0,8},{1,9},{2,10},{3,11},{4,12},{5,13},{6,14},{7,15},{8,0},{9,1},... | collective-permute-start | bytes 221192 | tf_op jit(solution)/shard_map/ppermute | solution.py:25
  306.3 5.3 %collective-permute-start.23 = (bf16[48,768]{1,0:T(8,128)(2,1)S(1)}, bf16[48,768]{1,0:T(8,128)(2,1)S(1)}, u32[]{:S(2)}, u32[]{:S(2)}) collective-permute-start(bf16[48,768]{1,0:T(8,128)(2,1)S(1)} %fusion.34), channel_id=1, source_target_pairs={{0,2},{1,3},{2,0},{3,1},{4,6},{5,7},{6,4},{7,5},{8,10},{9,11},{10,... | collective-permute-start | bytes 221192 | tf_op jit(solution)/shard_map/ppermute | solution.py:25
  307.9 6.1 %collective-permute-start.28 = (bf16[48,768]{1,0:T(8,128)(2,1)S(1)}, bf16[48,768]{1,0:T(8,128)(2,1)S(1)}, u32[]{:S(2)}, u32[]{:S(2)}) collective-permute-start(bf16[48,768]{1,0:T(8,128)(2,1)S(1)} %fusion.31), channel_id=1, source_target_pairs={{0,8},{1,9},{2,10},{3,11},{4,12},{5,13},{6,14},{7,15},{8,0},{9,1},... | collective-permute-start | bytes 221192 | tf_op jit(solution)/shard_map/ppermute | solution.py:25
  310.9 5.4 %collective-permute-start.19 = (bf16[48,768]{1,0:T(8,128)(2,1)S(1)}, bf16[48,768]{1,0:T(8,128)(2,1)S(1)}, u32[]{:S(2)}, u32[]{:S(2)}) collective-permute-start(bf16[48,768]{1,0:T(8,128)(2,1)S(1)} %fusion.39), channel_id=1, source_target_pairs={{0,16},{16,0},{1,17},{17,1},{2,18},{18,2},{3,19},{19,3},{4,20},{20... | collective-permute-start | bytes 221192 | tf_op jit(solution)/shard_map/ppermute | solution.py:25
  312.5 4.5 %collective-permute-start.24 = (bf16[48,768]{1,0:T(8,128)(2,1)S(1)}, bf16[48,768]{1,0:T(8,128)(2,1)S(1)}, u32[]{:S(2)}, u32[]{:S(2)}) collective-permute-start(bf16[48,768]{1,0:T(8,128)(2,1)S(1)} %fusion.36), channel_id=1, source_target_pairs={{0,16},{16,0},{1,17},{17,1},{2,18},{18,2},{3,19},{19,3},{4,20},{20... | collective-permute-start | bytes 221192 | tf_op jit(solution)/shard_map/ppermute | solution.py:25
  314.1 4.4 %collective-permute-start.29 = (bf16[48,768]{1,0:T(8,128)(2,1)S(1)}, bf16[48,768]{1,0:T(8,128)(2,1)S(1)}, u32[]{:S(2)}, u32[]{:S(2)}) collective-permute-start(bf16[48,768]{1,0:T(8,128)(2,1)S(1)} %fusion.33), channel_id=1, source_target_pairs={{0,16},{16,0},{1,17},{17,1},{2,18},{18,2},{3,19},{19,3},{4,20},{20... | collective-permute-start | bytes 221192 | tf_op jit(solution)/shard_map/ppermute | solution.py:25
  (48 other events, 562.1 us)
where the time goes:
time: 326 us; the launch traced here: 319 us
  Pallas kernels  129 us (40%)
  waiting for transfers between devices  72.7 us (22%)
  starting transfers between devices  55.4 us (17%)
  other arithmetic  36.9 us (11%)
  local copies, waits for them, and re-layouts  23.7 us (7%)
    pallas_call x11, Pallas kernels, call(): pl.pallas_call(wrapped, grid_spec=pltpu.PrefetchScalarGridSpec(num_scalar...  129 us
    ppermute x50, waiting for transfers between devices, flipped(): return lax.ppermute(value, axis, pairs)  72.7 us
    ppermute x50, starting transfers between devices, flipped(): return lax.ppermute(value, axis, pairs)  55.4 us
    convert_element_type x31, other arithmetic, added(): return total.astype(BF16)  30.5 us
    squeeze x12, local copies, waits for them, and re-layouts, step(): lax.index_in_dim(part, 0, dim, keepdims=False)  9.85 us
  transfers between devices with their start and end apart: 50, of which 17 were waited for; matrix products, arithmetic and copies ran while one was open for 16% of the time, Pallas kernels for 31%

commit v1 on v0

--- a/solution.py
+++ b/solution.py
@@ -2,6 +2,7 @@
 
 import jax
 import jax.numpy as jnp
+import numpy as np
 from jax import lax
 from jax.experimental import pallas as pl
 from jax.experimental.pallas import tpu as pltpu
@@ -44,39 +45,40 @@
 
 
 ANY = pl.BlockSpec(memory_space=pl.ANY)
-
-
-def call(kernel, scalars, operands, in_specs, out_specs, out_shape, grid, name, work, **more):
-    after = list(more.get("after", ()))
+LINE = []
+
+
+def call(kernel, scalars, operands, in_specs, out_specs, out_shape, grid, name, **more):
+    after = LINE[-1:]
     into = list(more.get("into", ()))
+    into_first = more.get("into_first", 0)
     scratch = list(more.get("scratch", ()))
-    taken, spare = len(operands), len(into) + len(after)
+    taken, spare, given = len(operands), len(into) + len(after), len(out_shape)
 
     def wrapped(scalars_ref, *refs):
-        kernel(scalars_ref, *refs[:taken], *refs[taken + spare :])
-
-    return pl.pallas_call(
+        outs = refs[taken + spare :]
+        kernel(scalars_ref, *refs[:taken], *outs[:given], *outs[given + 1 :])
+
+    outs = pl.pallas_call(
         wrapped,
         grid_spec=pltpu.PrefetchScalarGridSpec(
             num_scalar_prefetch=1,
             grid=grid,
             in_specs=list(in_specs) + [ANY] * spare,
-            out_specs=out_specs,
+            out_specs=list(out_specs) + [ANY],
             scratch_shapes=scratch,
         ),
-        out_shape=out_shape,
-        input_output_aliases={
-            1 + taken + i: i + more.get("into_first", 0) for i in range(len(into))
-        },
+        out_shape=list(out_shape) + [jax.ShapeDtypeStruct((8, 128), F32)],
+        input_output_aliases={1 + taken + i: i + into_first for i in range(len(into))},
         compiler_params=params(more.get("limit", VMEM_LIMIT)),
-        cost_estimate=pl.CostEstimate(
-            flops=int(work), bytes_accessed=more.get("moved", 2**20), transcendentals=0
-        ),
+        cost_estimate=pl.CostEstimate(flops=1, bytes_accessed=1, transcendentals=0),
         name=name,
     )(scalars, *operands, *into, *after)
-
-
-def gather_sent(scalars, rows, half, first, count, after=()):
+    LINE.append(outs[-1])
+    return list(outs[:-1])
+
+
+def gather_sent(scalars, rows, half, first, count):
     slot_rows, width = rows.shape[1:]
 
     def kernel(scalars_ref, rows_ref, out, sems):
@@ -97,18 +99,16 @@
         scalars,
         [rows],
         [ANY],
-        pl.BlockSpec(shape, lambda i, s: (0, 0, 0)),
-        jax.ShapeDtypeStruct(shape, rows.dtype),
+        [pl.BlockSpec(shape, lambda i, s: (0, 0, 0))],
+        [jax.ShapeDtypeStruct(shape, rows.dtype)],
         (1,),
         "gather_sent",
-        1e6,
         scratch=[pltpu.SemaphoreType.DMA((count,))],
-        after=after,
         limit=8 * 2**20,
-    )
-
-
-def scatter_home(scalars, kept, back, half, after=()):
+    )[0]
+
+
+def scatter_home(scalars, kept, back, half):
     slot_rows, width = kept.shape[1:]
 
     def kernel(scalars_ref, kept_ref, back_ref, out, sems):
@@ -135,15 +135,13 @@
         scalars,
         [kept, back],
         [ANY, ANY],
-        pl.BlockSpec(shape, lambda i, s: (0, 0, 0)),
-        jax.ShapeDtypeStruct(shape, kept.dtype),
+        [pl.BlockSpec(shape, lambda i, s: (0, 0, 0))],
+        [jax.ShapeDtypeStruct(shape, kept.dtype)],
         (1,),
         "scatter_home",
-        1e6,
         scratch=[pltpu.SemaphoreType.DMA((2, half))],
-        after=after,
         limit=8 * 2**20,
-    )
+    )[0]
 
 
 def split_heads(value):
@@ -182,7 +180,7 @@
 
 
 def attention_forward(
-    scalars, rows, received, live, weights, first, half, into=(), after=()
+    scalars, rows, received, live, weights, first, half, into=()
 ):
     w_qkv, b_qv, w_out, norm_gains, bias_rows = weights
     slot_rows, width = rows.shape[1:]
@@ -284,10 +282,7 @@
         ],
         (pairs // 2,),
         "attention_forward",
-        pairs * length * width * width * 10,
         into=into,
-        after=after,
-        moved=12 * 2**20,
     )
 
 
@@ -299,7 +294,7 @@
             out[j] = grad[pl.ds(pl.multiple_of((row + which) * shard, 16), shard), :]
 
 
-def feed_forward(scalars, normed, cot, far_cot, weights, half, shards, base, after=()):
+def feed_forward(scalars, normed, cot, far_cot, weights, half, shards, base):
     w_in, b_in, w_back, norm_gains, bias_rows = weights
     slot_rows, width = cot.shape[1:]
     inner_width = w_in.shape[1]
@@ -475,8 +470,6 @@
         ],
         (steps + parts,),
         "feed_forward",
-        height * width * inner_width * 6,
-        after=after,
         scratch=[
             pltpu.VMEM((width, inner_width), BF16),
             pltpu.VMEM((inner_width, width), BF16),
@@ -487,11 +480,10 @@
             pltpu.VMEM((part, width - left), BF16),
             pltpu.SemaphoreType.DMA((2, chunks)),
         ],
-        moved=28 * 2**20,
-    )
-
-
-def feed_backward(scalars, branch, slope, normed, root, context, weights, shards, base, after=()):
+    )
+
+
+def feed_backward(scalars, branch, slope, normed, root, context, weights, shards, base):
     w_in, w_back, norm_gains, bias_rows = weights
     total, width = branch.shape
     inner_width = slope.shape[1]
@@ -616,18 +608,15 @@
         ],
         (steps,),
         "feed_backward",
-        total * width * inner_width * 6,
-        after=after,
         scratch=[
             pltpu.VMEM((total, width), F32),
             pltpu.VMEM((total, width), BF16),
             pltpu.VMEM((width, chunk), BF16),
         ],
-        moved=26 * 2**20,
-    )
-
-
-def attention_backward(scalars, kept, weights, part, parts, shards, base, into=(), after=()):
+    )
+
+
+def attention_backward(scalars, kept, weights, part, parts, shards, base, into=()):
     low_attn, mixed, probs, joined = kept
     w_out, w_qkv = weights
     total, width = low_attn.shape
@@ -755,52 +744,173 @@
         out_shape,
         (steps,),
         "attention_backward",
-        total // parts * width * width * 20,
         into=into[1:],
         into_first=1,
-        after=after,
         scratch=scratch,
-        moved=12 * 2**20,
-    )
-
-
-def added(parts):
-    total = parts[0].astype(F32)
-    for part in parts[1:]:
-        total = total + part.astype(F32)
-    return total.astype(BF16)
+    )
 
 
 class Shards:
     def __init__(self, send, keep, order):
         places, self.shard, self.width = send.shape
         bits = places.bit_length() - 1
-        self.shape = (2,) * bits + (self.shard, self.width)
         self.order = list(order)
-        self.left = list(range(bits))[::-1]
+        self.places = list(range(bits))[::-1]
+        shape = (2,) * bits + (self.shard, self.width)
+        self.held = [(keep.reshape(shape), self.places)]
+        self.coming = flipped(send, "dp", 1).reshape(shape)
+        self.done = ()
         self.mine = None
-        self.held = [keep.reshape(self.shape)]
-        self.coming = flipped(send, "dp", 1).reshape(self.shape)
-
-    def step(self, after=None):
-        coming = self.coming
-        if after is not None:
-            coming, _ = lax.optimization_barrier((coming, after))
-        self.held.append(coming)
-        if not self.order:
-            self.mine = lax.optimization_barrier(added(self.held))
-            self.coming = flipped(self.mine, "mod", 1)
-            return self.mine
-        bit = self.order.pop(0)
-        dim = self.left.index(bit)
-        away = added([lax.index_in_dim(part, 1, dim, keepdims=False) for part in self.held])
-        self.held = [lax.index_in_dim(part, 0, dim, keepdims=False) for part in self.held]
-        self.left.remove(bit)
-        self.coming = flipped(away, "dp", 2 << bit)
-        return away
-
-    def result(self):
-        return self.mine.astype(F32) + self.coming.astype(F32)
+
+    def plan(self):
+        self.held.append((self.coming, self.places))
+        bit = self.order[0] if self.order else None
+        rest = [each for each in self.places if each != bit]
+        operands, specs, entries = [], [], []
+        for array, dims in self.held:
+            place = tuple(1 if dim == bit else 0 for dim in dims)
+            block = tuple(2 if dim in rest else 1 for dim in dims)
+            operands.append(array)
+            specs.append(
+                pl.BlockSpec(
+                    block + (self.shard, self.width), lambda i, s, place=place: place + (0, 0)
+                )
+            )
+            entries.append([rest.index(dim) if dim in rest else None for dim in dims])
+        shape = (2,) * len(rest) + (self.shard, self.width)
+        return operands, specs, entries, shape
+
+    def sent(self, total):
+        if self.order:
+            bit = self.order.pop(0)
+            self.places = [each for each in self.places if each != bit]
+            self.coming = flipped(total, "dp", 2 << bit)
+        else:
+            self.mine = total
+            self.coming = flipped(total, "mod", 1)
+
+
+class Everywhere:
+    def __init__(self, mine, masks):
+        self.masks = list(masks)
+        self.send(mine)
+
+    def send(self, mine):
+        self.mine = mine
+        if self.masks:
+            self.coming = flipped(mine, "dp", self.masks.pop(0))
+        else:
+            self.coming = flipped(mine, "mod", 1)
+
+
+def advance(scalars, pieces, extra=None):
+    plans = [piece.plan() for piece in pieces]
+    operands = [array for plan in plans for array in plan[0]]
+    in_specs = [spec for plan in plans for spec in plan[1]]
+    shapes = [plan[3] for plan in plans]
+    out_shape = [jax.ShapeDtypeStruct(shape, BF16) for shape in shapes]
+    if extra is not None:
+        operands += [extra.mine, extra.coming]
+        in_specs += [whole(extra.mine)] * 2
+        out_shape.append(jax.ShapeDtypeStruct(extra.mine.shape, F32))
+
+    def kernel(scalars_ref, *refs):
+        ins, outs = refs[: len(operands)], refs[len(operands) :]
+        at = 0
+        for plan, out in zip(plans, outs):
+            entries, shape = plan[2], plan[3]
+            for index in np.ndindex(shape[:-2]):
+                total = None
+                for n, dims in enumerate(entries):
+                    where = tuple(0 if dim is None else index[dim] for dim in dims)
+                    term = ins[at + n][where].astype(F32)
+                    total = term if total is None else total + term
+                out[index] = total.astype(BF16)
+            at += len(entries)
+        if extra is not None:
+            outs[-1][...] = ins[at][...] + ins[at + 1][...]
+
+    def full(shape):
+        return pl.BlockSpec(shape, lambda i, s: (0,) * len(shape))
+
+    totals = call(
+        kernel,
+        scalars,
+        operands,
+        in_specs,
+        [full(shape.shape) for shape in out_shape],
+        out_shape,
+        (1,),
+        "advance",
+    )
+    for piece, total in zip(pieces, totals):
+        piece.sent(total)
+    if extra is not None:
+        extra.send(totals[-1])
+
+
+def finish(scalars, pieces, extra=None):
+    operands, widths = [], []
+    for piece in pieces:
+        operands += [piece.mine, piece.coming]
+        widths.append(piece.width)
+    if extra is not None:
+        operands += [extra.mine, extra.coming]
+    shape = (pieces[0].shard, sum(widths))
+    out_shape = [jax.ShapeDtypeStruct(shape, F32)]
+    if extra is not None:
+        out_shape.append(jax.ShapeDtypeStruct(extra.mine.shape, F32))
+
+    def kernel(scalars_ref, *refs):
+        out = refs[len(operands)]
+        first = 0
+        for n, width in enumerate(widths):
+            out[:, first : first + width] = refs[2 * n][...].astype(F32) + refs[
+                2 * n + 1
+            ][...].astype(F32)
+            first += width
+        if extra is not None:
+            refs[-1][...] = refs[2 * len(widths)][...] + refs[2 * len(widths) + 1][...]
+
+    return call(
+        kernel,
+        scalars,
+        operands,
+        [whole(array) for array in operands],
+        [pl.BlockSpec(each.shape, lambda i, s: (0, 0)) for each in out_shape],
+        out_shape,
+        (1,),
+        "finish",
+    )
+
+
+def pack_small(scalars, sums_qv_a, sums_qv_b, sums_one, sums_two, inner_sum):
+    width = sums_one.shape[1]
+    count = inner_sum.shape[1] // width
+
+    def kernel(scalars_ref, qv_a, qv_b, one, two, inner, out):
+        out[0:2] = qv_a[0:2] + qv_b[0:2]
+        out[2:3] = one[0:1]
+        out[3:4] = two[0:1]
+        out[4:5] = one[2:3]
+        out[5:6] = one[1:2]
+        out[6:7] = two[2:3]
+        out[7:8] = two[1:2]
+        for i in range(count):
+            out[8 + i : 9 + i] = inner[0:1, i * width : (i + 1) * width]
+
+    operands = [sums_qv_a, sums_qv_b, sums_one, sums_two, inner_sum]
+    shape = (8 + count, width)
+    return call(
+        kernel,
+        scalars,
+        operands,
+        [whole(array) for array in operands],
+        [pl.BlockSpec(shape, lambda i, s: (0, 0))],
+        [jax.ShapeDtypeStruct(shape, F32)],
+        (1,),
+        "pack_small",
+    )[0]
 
 
 def reduce_plain(send, keep):
@@ -808,17 +918,6 @@
     total = total.reshape(-1, total.shape[-1]).astype(F32)
     share = lax.psum_scatter(total, "dp", scatter_dimension=0, tiled=True)
     return lax.psum(share.astype(BF16), "mod").astype(F32)
-
-
-def sum_everywhere(value):
-    shards = lax.axis_size("dp")
-    if shards & (shards - 1):
-        return lax.psum(value, ("mod", "dp"))
-    mask = 1
-    while mask < shards:
-        value = value + flipped(value, "dp", mask)
-        mask *= 2
-    return value + flipped(value, "mod", 1)
 
 
 def body(
@@ -839,7 +938,7 @@
     place = lax.axis_index("dp")
     shards = lax.axis_size("dp")
     groups = partner.shape[1]
-    aligned = shards >= 8 and shards & (shards - 1) == 0 and (layer_rows.shape[2] // shards) % 16 == 0
+    aligned = shards == 16 and (layer_rows.shape[2] // shards) % 16 == 0
     layout = shards if aligned else 16
     half = groups // 2
     width = layer_rows.shape[2]
@@ -853,11 +952,12 @@
         [partner[0], jnp.stack([side, spot & 1, spot >> 1]).astype(jnp.int32)]
     )
     cut = half // 2
+    LINE.clear()
     sent_a = gather_sent(scalars, rows, half, 0, cut)
     got_a = flipped(sent_a, "mod", 1)
-    sent_b = gather_sent(scalars, rows, half, cut, cut, [sent_a])
+    sent_b = gather_sent(scalars, rows, half, cut, cut)
     got_b = flipped(sent_b, "mod", 1)
-    sent_cot = gather_sent(scalars, cot, half, 0, half, [sent_b])
+    sent_cot = gather_sent(scalars, cot, half, 0, half)
     far_cot = flipped(sent_cot, "mod", 1)
 
     live = row_live.reshape(2, groups, slot_rows)
@@ -873,88 +973,75 @@
     )[:, None, :]
 
     heads_weights = (w_qkv, b_qv, w_out, norm_gains, bias_rows)
-    first_part = attention_forward(
-        scalars, rows, got_a, seen, heads_weights, 0, half, after=[sent_cot]
-    )
+    first_part = attention_forward(scalars, rows, got_a, seen, heads_weights, 0, half)
     joined, mixed, probs, context, normed, root = attention_forward(
         scalars, rows, got_b, seen, heads_weights, cut, half, into=first_part
     )
     feed_weights = (w_in, b_in.reshape(1, inner_width), w_back, norm_gains, bias_rows)
-    slope, branch, out_kept, out_far, sums_two, *grads = feed_forward(
+    slope, branch, out_kept, out_far, sums_two, *back = feed_forward(
         scalars, normed, cot, far_cot, feed_weights, half, layout, groups
     )
+    out_back = flipped(out_far, "mod", 1)
     back_weights = (w_in, w_back, norm_gains, bias_rows)
+    attn_weights = (w_out, w_qkv)
     bits = (layout // 2).bit_length() - 1
     order = list(range(bits))
     other = order[1:] + order[:1]
-
-    def travel(send, keep, steps):
-        return Shards(send, keep, steps) if aligned else (send, keep)
-
-    def steps_of(pieces, after):
-        return [piece.step(after) for piece in pieces] if aligned else []
-
-    back = [travel(*grads[0:2], order), travel(*grads[2:4], order)]
-    sent = steps_of(back[:1], grads[0]) + steps_of(back[1:], grads[0])
-    out_back = flipped(out_far, "mod", 1)
-    low_attn, sums_one, inner_sum, *grads = feed_backward(
-        scalars, branch, slope, normed, root, context, back_weights, layout, groups, after=sent
-    )
-    inner = [travel(*grads[0:2], order), travel(*grads[2:4], order)]
-    outer = travel(*grads[4:6], other)
-    sent = steps_of(back, low_attn) + steps_of(inner, low_attn) + steps_of([outer], low_attn)
+    if aligned:
+        back_a, back_b = Shards(*back[:2], order), Shards(*back[2:], order)
+        advance(scalars, [back_a])
+        advance(scalars, [back_b])
+    low_attn, sums_one, inner_sum, *inner = feed_backward(
+        scalars, branch, slope, normed, root, context, back_weights, layout, groups
+    )
+    if aligned:
+        inner_a, inner_b = Shards(*inner[:2], order), Shards(*inner[2:4], order)
+        outer = Shards(*inner[4:], other)
+    out_rows = scatter_home(scalars, out_kept, out_back, half).reshape(1, -1, width)
+    if aligned:
+        advance(scalars, [inner_a])
+        advance(scalars, [inner_b, outer])
+        advance(scalars, [back_a, back_b])
     attn_kept = (low_attn, mixed, probs, joined)
-    attn_weights = (w_out, w_qkv)
     *first_part, sums_qv_a = attention_backward(
-        scalars, attn_kept, attn_weights, 0, 2, layout, groups, after=sent
-    )
-    sent = steps_of(back + [outer], sums_qv_a)
-    _, d_kept, d_far, sums_qv_b, *grads = attention_backward(
-        scalars, attn_kept, attn_weights, 1, 2, layout, groups, into=first_part, after=sent
-    )
-    qkv = [
-        travel(*grads[0:2], order),
-        travel(*grads[2:4], other),
-        travel(*grads[4:6], order),
-    ]
+        scalars, attn_kept, attn_weights, 0, 2, layout, groups
+    )
+    if aligned:
+        advance(scalars, [back_a, back_b, outer])
+    _, d_kept, d_far, sums_qv_b, *qkv = attention_backward(
+        scalars, attn_kept, attn_weights, 1, 2, layout, groups, into=first_part
+    )
     d_back = flipped(d_far, "mod", 1)
-    pieces = back + inner + [outer] + qkv
+    small = pack_small(scalars, sums_qv_a, sums_qv_b, sums_one, sums_two, inner_sum)
     if aligned:
-        steps_of(back + inner + [outer], sums_qv_b)
-        while any(piece.mine is None for piece in pieces):
-            for piece in pieces:
-                if piece.mine is None:
-                    piece.step()
-        done = [piece.result() for piece in pieces]
+        qkv_a, qkv_b = Shards(*qkv[:2], order), Shards(*qkv[2:4], other)
+        qkv_c = Shards(*qkv[4:], order)
+        small = Everywhere(small, [1] + [2 << bit for bit in order])
+        advance(scalars, [inner_a, inner_b, back_a, back_b, outer])
+        advance(scalars, [qkv_a, qkv_b, qkv_c], small)
+        advance(scalars, [inner_a, inner_b, outer])
+        (grad_back,) = finish(scalars, [back_a, back_b])
+        advance(scalars, [qkv_a, qkv_b, qkv_c], small)
+        advance(scalars, [inner_a, inner_b])
+        grad_rows = scatter_home(scalars, d_kept, d_back, half).reshape(1, -1, width)
+        advance(scalars, [qkv_a, qkv_b, qkv_c], small)
+        (grad_out,) = finish(scalars, [outer])
+        (grad_in,) = finish(scalars, [inner_a, inner_b])
+        advance(scalars, [qkv_a, qkv_b, qkv_c], small)
+        grad_qkv, small = finish(scalars, [qkv_a, qkv_b, qkv_c], small)
     else:
-        done = [reduce_plain(*piece) for piece in pieces]
-    grad_back = jnp.concatenate(done[0:2], 1)
-    grad_in = jnp.concatenate(done[2:4], 1)
-    grad_out = done[4]
-    grad_qkv = jnp.concatenate(done[5:], 1)
-
-    sums_qv = sums_qv_a + sums_qv_b
-    small = jnp.concatenate(
-        [
-            sums_qv[0:2],
-            sums_one[0:1],
-            sums_two[0:1],
-            sums_one[2:3],
-            sums_one[1:2],
-            sums_two[2:3],
-            sums_two[1:2],
-            inner_sum[0].reshape(-1, width),
-        ],
-        0,
-    )
-    small = sum_everywhere(small)
+        grad_back = jnp.concatenate([reduce_plain(*back[:2]), reduce_plain(*back[2:])], 1)
+        grad_in = jnp.concatenate([reduce_plain(*inner[:2]), reduce_plain(*inner[2:4])], 1)
+        grad_out = reduce_plain(*inner[4:])
+        grad_qkv = jnp.concatenate([reduce_plain(*qkv[i : i + 2]) for i in (0, 2, 4)], 1)
+        grad_rows = scatter_home(scalars, d_kept, d_back, half).reshape(1, -1, width)
+        small = lax.psum(small, ("mod", "dp"))
+
     shard = width // shards
     rows_small = lax.dynamic_slice_in_dim(small[:8], place * shard, shard, 1)
     inner_shard = inner_width // shards
     grad_b_in = lax.dynamic_slice_in_dim(small[8:].reshape(-1), place * inner_shard, inner_shard)
 
-    out_rows = scatter_home(scalars, out_kept, out_back, half).reshape(1, -1, width)
-    grad_rows = scatter_home(scalars, d_kept, d_back, half).reshape(1, -1, width)
     return (
         out_rows,
         grad_rows,

time: 326 us -> 336 us (1.031)
  Pallas kernels: 129 us -> 181 us
  other arithmetic: 36.9 us -> 1.49 us
  starting transfers between devices: 55.4 us -> 49.6 us
    pallas_call x11 -> x29, Pallas kernels: 129 us -> 181 us  [call(): pl.pallas_call(wrapped, grid_spec=pltpu.PrefetchScalarGridSpec(num_scalar...]
    convert_element_type x31 -> x0, other arithmetic: 30.5 us -> none  [added(): return total.astype(BF16)]
    unnamed x92 -> x136, local copies, waits for them, and re-layouts: 5.45 us -> 16.8 us
    squeeze x12 -> x0, local copies, waits for them, and re-layouts: 9.85 us -> none  [step(): lax.index_in_dim(part, 0, dim, keepdims=False)]
    ppermute x50, starting transfers between devices: 55.4 us -> 49.6 us  [flipped(): return lax.ppermute(value, axis, pairs)]
    slice x3 -> x0, local copies, waits for them, and re-layouts: 3.88 us -> none  [the longest x1 1.49 us: body(): sums_one[1:2]]
  transfers between devices with their start and end apart: 50 -> 50, of which waited for: 17 -> 12; matrix products, arithmetic and copies ran while one was open for 16% -> 0% of each run, Pallas kernels for 31% -> 42%
where the time goes in v1:
time: 336 us; the launch traced here: 330 us
  Pallas kernels  181 us (54%)
  waiting for transfers between devices  75.3 us (22%)
  starting transfers between devices  49.6 us (15%)
  local copies, waits for them, and re-layouts  20.9 us (6%)
    pallas_call x29, Pallas kernels, call(): pl.pallas_call(wrapped, grid_spec=pltpu.PrefetchScalarGridSpec(num_scalar...  181 us
    ppermute x50, waiting for transfers between devices, flipped(): return lax.ppermute(value, axis, pairs)  75.3 us
    ppermute x50, starting transfers between devices, flipped(): return lax.ppermute(value, axis, pairs)  49.6 us
    unnamed x136, local copies, waits for them, and re-layouts  16.8 us
  transfers between devices with their start and end apart: 50, of which 12 were waited for; matrix products, arithmetic and copies ran while one was open for 0% of the time, Pallas kernels for 42%

profile of v1, /device:TPU:0, one launch (start us, length us, event | category | flops | bytes accessed | tf_op | source)
XLA Modules:
  0.0 329.9 jit_solution(7690077759395267158)
XLA Ops:
  5.1 1.7 gather_sent.5
  7.3 2.9 collective-permute-start.2
  10.3 2.0 collective-permute-start.1
  13.8 30.9 %collective-permute-done.1.refs_2_ = bf16[4,64,768]{2,1,0:T(8,128)(2,1)S(1)} collective-permute-done((bf16[4,64,768]{2,1,0:T(8,128)(2,1)S(1)}, bf16[4,64,768]{2,1,0:T(8,128)(2,1)S(1)}, u32[]{:S(2)}, u32[]{:S(2)}) %collective-permute-start.1) | collective-permute-done | bytes 393248 | tf_op jit(solution)/shard_map/ppermute | solution.py:26
  45.4 10.1 %attention_forward.2 = (bf16[1024,768]{1,0:T(8,128)(2,1)}, bf16[1024,2304]{1,0:T(8,128)(2,1)}, bf16[8,6,256,128]{3,2,1,0:T(8,128)(2,1)}, bf16[1024,768]{1,0:T(8,...) custom-call(s32[19]{0:T(128)} %copy-done.4, bf16[16,64,768]{2,1,0:T(8,128)(2,1)} %bitcast.34, ...), custom_call_target="tpu_custom_call" | custom-call | flops 1 | bytes 1 | tf_op jit(solution)/shard_map/attention_forward/pallas_call | solution.py:62
  56.3 10.2 %attention_forward.3 = (bf16[1024,768]{1,0:T(8,128)(2,1)}, bf16[1024,2304]{1,0:T(8,128)(2,1)}, bf16[8,6,256,128]{3,2,1,0:T(8,128)(2,1)}, bf16[1024,768]{1,0:T(8,...) custom-call(s32[19]{0:T(128)} %copy-done.4, ...), custom_call_target="tpu_custom_call", output_to_operand_aliasing={{0}: (10, {}), {1}: (11, {}), {2}: (12, {}), {3}: (13, {}),... | custom-call | flops 1 | bytes 1 | tf_op jit(solution)/shard_map/attention_forward/pallas_call | solution.py:62
  67.4 29.5 %feed_forward.1 = (bf16[1024,3072]{1,0:T(8,128)(2,1)}, bf16[1024,768]{1,0:T(8,128)(2,1)}, bf16[8,64,768]{2,1,0:T(8,128)(2,1)}, bf16[8,64,768]{2,1,0:T(8,128)(2,1...) custom-call(s32[19]{0:T(128)} %copy-done.4, ...), custom_call_target="tpu_custom_call" | custom-call | flops 1 | bytes 1 | tf_op jit(solution)/shard_map/feed_forward/pallas_call | solution.py:62
  97.5 1.8 collective-permute-start.3
  101.1 2.9 advance.13
  105.0 2.9 advance.14
  107.8 27.8 %feed_backward.1 = (bf16[1024,768]{1,0:T(8,128)(2,1)}, f32[8,768]{1,0:T(8,128)}, f32[8,3072]{1,0:T(8,128)}, bf16[8,48,1536]{2,1,0:T(8,128)(2,1)}, bf16[8,48,1536...) custom-call(s32[19]{0:T(128)} %copy-done.4, ...), custom_call_target="tpu_custom_call" | custom-call | flops 1 | bytes 1 | tf_op jit(solution)/shard_map/feed_backward/pallas_call | solution.py:62
  136.3 1.8 collective-permute-start.6
  139.1 3.9 %scatter_home.2 = (bf16[16,64,768]{2,1,0:T(8,128)(2,1)}, f32[8,128]{1,0:T(8,128)S(1)}) custom-call(s32[19]{0:T(128)S(1)} %copy-done.5, bf16[8,64,768]{2,1,0:T(8,128)(2,1)S(1)} %copy-done.3, bf16[8,64,768]{2,1,0:T(8,128)(2,1)S(1)} %collective-permute-done.3.refs_1_, f32[8,128]{1,0:T(8,128)S(1)} %copy-done.8), custom_call_target="tpu_custom_call" | custom-call | flops 1 | bytes 1 | tf_op jit(solution)/shard_map/scatter_home/pallas_call | solution.py:62
  144.0 2.9 advance.15
  148.2 3.1 advance.16
  152.5 12.1 %collective-permute-done.7.refs_5_.refs_6_.refs_13_ = bf16[2,2,192,384]{3,2,1,0:T(8,128)(2,1)S(1)} collective-permute-done((bf16[2,2,192,384]{3,2,1,0:T(8,128)(2,1)S(1)}, bf16[2,2,192,384]{3,2,1,0:T(8,128)(2,1)S(1)}, u32[]{:S(2)}, u32[]{:S(2)}) %collective-permute-start.7) | collective-permute-done | bytes 589856 | tf_op jit(solution)/shard_map/ppermute | solution.py:26
  165.4 3.2 advance.17
  168.6 1.8 collective-permute-start.11
  170.7 1.8 collective-permute-start.13
  174.6 16.6 %attention_backward.2 = (bf16[1024,2304]{1,0:T(8,128)(2,1)}, bf16[8,64,768]{2,1,0:T(8,128)(2,1)}, bf16[8,64,768]{2,1,0:T(8,128)(2,1)}, f32[8,768]{1,0:T(8,128)}, f32[8,128]{1,0:T(8,128)}) custom-call(s32[19]{0:T(128)} %copy-done.4, bf16[1024,768]{1,0:T(8,128)(2,1)} %get-tuple-element.158.refs_0_, bf16[1024,2304]{1,0:T(8,128)(2,1)} %get-tuple-element.159.refs_1_, ...), custom_call_target="tpu_custom_call" | custom-call | flops 1 | bytes 1 | tf_op jit(solution)/shard_map/attention_backward/pallas_call | solution.py:62
  192.1 3.0 advance.18
  195.1 2.6 collective-permute-start.17
  198.1 2.6 collective-permute-start.19
  200.6 23.5 %attention_backward.3 = (bf16[256,2304]{1,0:T(8,128)(2,1)}, bf16[8,64,768]{2,1,0:T(8,128)(2,1)}, bf16[8,64,768]{2,1,0:T(8,128)(2,1)}, f32[8,768]{1,0:T(8,128)}, ...) custom-call(s32[19]{0:T(128)} %copy-done.4, ...), custom_call_target="tpu_custom_call", output_to_operand_aliasing={{1}: (8, {}), {2}: (9, {})} | custom-call | flops 1 | bytes 1 | tf_op jit(solution)/shard_map/attention_backward/pallas_call | solution.py:62
  224.9 2.3 pack_small.1
  229.1 3.8 %advance.19 = (bf16[2,48,1536]{2,1,0:T(8,128)(2,1)}, bf16[2,48,1536]{2,1,0:T(8,128)(2,1)}, bf16[192,384]{1,0:T(8,128)(2,1)}, bf16[192,384]{1,0:T(8,128)(2,1)}, b...) custom-call(s32[19]{0:T(128)} %copy-done.4, bf16[2,2,2,48,1536]{4,3,2,1,0:T(8,128)(2,1)} %bitcast.68, ...), custom_call_target="tpu_custom_call" | custom-call | flops 1 | bytes 1 | tf_op jit(solution)/shard_map/advance/pallas_call | solution.py:62
  232.9 1.6 collective-permute-start.22
  234.4 3.0 collective-permute-done.22.refs_12_
  240.0 1.5 collective-permute-start.21
  241.6 3.1 advance.20
  244.6 6.7 %collective-permute-done.33.refs_1_ = bf16[192,384]{1,0:T(8,128)(2,1)S(1)} collective-permute-done((bf16[192,384]{1,0:T(8,128)(2,1)}, bf16[192,384]{1,0:T(8,128)(2,1)S(1)}, u32[]{:S(2)}, u32[]{:S(2)}) %collective-permute-start.33) | collective-permute-done | bytes 147488 | tf_op jit(solution)/shard_map/ppermute | solution.py:26
  256.4 2.9 advance.21
  259.3 6.9 %collective-permute-done.32.refs_10_ = f32[12,768]{1,0:T(8,128)S(1)} collective-permute-done((f32[12,768]{1,0:T(8,128)}, f32[12,768]{1,0:T(8,128)S(1)}, u32[]{:S(2)}, u32[]{:S(2)}) %collective-permute-start.32) | collective-permute-done | bytes 36896 | tf_op jit(solution)/shard_map/ppermute | solution.py:26
  266.6 2.6 collective-permute-start.28
  269.2 2.7 finish.4
  272.7 2.9 advance.22
  276.4 3.1 collective-permute-done.27.refs_4_
  279.5 4.3 %collective-permute-done.28.refs_9_ = bf16[48,1536]{1,0:T(8,128)(2,1)S(1)} collective-permute-done((bf16[48,1536]{1,0:T(8,128)(2,1)}, bf16[48,1536]{1,0:T(8,128)(2,1)S(1)}, u32[]{:S(2)}, u32[]{:S(2)}) %collective-permute-start.28) | collective-permute-done | bytes 147488 | tf_op jit(solution)/shard_map/ppermute | solution.py:26
  284.5 3.1 advance.23
  293.4 3.9 %scatter_home.3 = (bf16[16,64,768]{2,1,0:T(8,128)(2,1)}, f32[8,128]{1,0:T(8,128)S(1)}) custom-call(s32[19]{0:T(128)S(1)} %copy-done.6, bf16[8,64,768]{2,1,0:T(8,128)(2,1)S(1)} %copy-done.2, bf16[8,64,768]{2,1,0:T(8,128)(2,1)S(1)} %collective-permute-done.14.refs_1_, f32[8,128]{1,0:T(8,128)S(1)} %copy-done.9), custom_call_target="tpu_custom_call" | custom-call | flops 1 | bytes 1 | tf_op jit(solution)/shard_map/scatter_home/pallas_call | solution.py:62
  298.6 2.7 advance.24
  301.3 1.6 collective-permute-start.40
  302.9 2.9 collective-permute-start.41
  305.8 2.3 finish.5
  308.8 2.7 finish.6
  312.1 2.8 advance.25
  319.0 3.8 %collective-permute-done.49.refs_7_ = f32[12,768]{1,0:T(8,128)S(1)} collective-permute-done((f32[12,768]{1,0:T(8,128)}, f32[12,768]{1,0:T(8,128)S(1)}, u32[]{:S(2)}, u32[]{:S(2)}) %collective-permute-start.49) | collective-permute-done | bytes 36896 | tf_op jit(solution)/shard_map/ppermute | solution.py:26
  323.5 2.5 finish.7
  (233 shorter events, 51.2 us)
Async XLA Ops:
  7.3 59.2 %collective-permute-start.2 = (bf16[8,64,768]{2,1,0:T(8,128)(2,1)S(1)}, bf16[8,64,768]{2,1,0:T(8,128)(2,1)S(1)}, u32[]{:S(2)}, u32[]{:S(2)}) collective-permute-start(bf16[8,64,768]{2,1,0:T(8,128)(2,1)S(1)} %get-tuple-element.141), channel_id=1, source_target_pairs={{0,16},{16,0},{1,17},{17,1},{2,18},{18,2},{3,19},{19,3},{4,20},{20... | collective-permute-start | bytes 2359304 | tf_op jit(solution)/shard_map/ppermute | solution.py:26
  10.3 45.3 %collective-permute-start = (bf16[4,64,768]{2,1,0:T(8,128)(2,1)S(1)}, bf16[4,64,768]{2,1,0:T(8,128)(2,1)S(1)}, u32[]{:S(2)}, u32[]{:S(2)}) collective-permute-start(bf16[4,64,768]{2,1,0:T(8,128)(2,1)S(1)} %get-tuple-element.129), channel_id=1, source_target_pairs={{0,16},{16,0},{1,17},{17,1},{2,18},{18,2},{3,19},{19,3},{4,20},{20... | collective-permute-start | bytes 1179656 | tf_op jit(solution)/shard_map/ppermute | solution.py:26
  10.3 34.4 %collective-permute-start.1 = (bf16[4,64,768]{2,1,0:T(8,128)(2,1)S(1)}, bf16[4,64,768]{2,1,0:T(8,128)(2,1)S(1)}, u32[]{:S(2)}, u32[]{:S(2)}) collective-permute-start(bf16[4,64,768]{2,1,0:T(8,128)(2,1)S(1)} %get-tuple-element.130), channel_id=1, source_target_pairs={{0,16},{16,0},{1,17},{17,1},{2,18},{18,2},{3,19},{19,3},{4,20},{20... | collective-permute-start | bytes 1179656 | tf_op jit(solution)/shard_map/ppermute | solution.py:26
  97.0 6.9 %collective-permute-start.4 = (bf16[8,192,384]{2,1,0:T(8,128)(2,1)}, bf16[8,192,384]{2,1,0:T(8,128)(2,1)S(1)}, u32[]{:S(2)}, u32[]{:S(2)}) collective-permute-start(bf16[8,192,384]{2,1,0:T(8,128)(2,1)} %get-tuple-element.150), channel_id=1, source_target_pairs={{0,1},{1,0},{2,3},{3,2},{4,5},{5,4},{6,7},{7,6},{8,9},{9,8},{10,11... | collective-permute-start | bytes 3538952 | tf_op jit(solution)/shard_map/ppermute | solution.py:26
  97.5 40.6 %collective-permute-start.3 = (bf16[8,64,768]{2,1,0:T(8,128)(2,1)}, bf16[8,64,768]{2,1,0:T(8,128)(2,1)S(1)}, u32[]{:S(2)}, u32[]{:S(2)}) collective-permute-start(bf16[8,64,768]{2,1,0:T(8,128)(2,1)} %get-tuple-element.144), channel_id=1, source_target_pairs={{0,16},{16,0},{1,17},{17,1},{2,18},{18,2},{3,19},{19,3},{4,20},{20... | collective-permute-start | bytes 2359304 | tf_op jit(solution)/shard_map/ppermute | solution.py:26
  135.6 7.4 %collective-permute-start.10 = (bf16[8,48,1536]{2,1,0:T(8,128)(2,1)}, bf16[8,48,1536]{2,1,0:T(8,128)(2,1)S(1)}, u32[]{:S(2)}, u32[]{:S(2)}) collective-permute-start(bf16[8,48,1536]{2,1,0:T(8,128)(2,1)} %get-tuple-element.169), channel_id=1, source_target_pairs={{0,1},{1,0},{2,3},{3,2},{4,5},{5,4},{6,7},{7,6},{8,9},{9,8},{10,11... | collective-permute-start | bytes 3538952 | tf_op jit(solution)/shard_map/ppermute | solution.py:26
  135.8 11.1 %collective-permute-start.8 = (bf16[8,48,1536]{2,1,0:T(8,128)(2,1)}, bf16[8,48,1536]{2,1,0:T(8,128)(2,1)S(1)}, u32[]{:S(2)}, u32[]{:S(2)}) collective-permute-start(bf16[8,48,1536]{2,1,0:T(8,128)(2,1)} %get-tuple-element.165), channel_id=1, source_target_pairs={{0,1},{1,0},{2,3},{3,2},{4,5},{5,4},{6,7},{7,6},{8,9},{9,8},{10,11... | collective-permute-start | bytes 3538952 | tf_op jit(solution)/shard_map/ppermute | solution.py:26
  136.2 10.7 %collective-permute-start.9 = (bf16[8,48,768]{2,1,0:T(8,128)(2,1)}, bf16[8,48,768]{2,1,0:T(8,128)(2,1)S(1)}, u32[]{:S(2)}, u32[]{:S(2)}) collective-permute-start(bf16[8,48,768]{2,1,0:T(8,128)(2,1)} %get-tuple-element.167), channel_id=1, source_target_pairs={{0,1},{1,0},{2,3},{3,2},{4,5},{5,4},{6,7},{7,6},{8,9},{9,8},{10,11... | collective-permute-start | bytes 1769480 | tf_op jit(solution)/shard_map/ppermute | solution.py:26
  136.3 16.2 %collective-permute-start.6 = (bf16[2,2,192,384]{3,2,1,0:T(8,128)(2,1)S(1)}, bf16[2,2,192,384]{3,2,1,0:T(8,128)(2,1)S(1)}, u32[]{:S(2)}, u32[]{:S(2)}) collective-permute-start(bf16[2,2,192,384]{3,2,1,0:T(8,128)(2,1)S(1)} %copy-done.65), channel_id=1, source_target_pairs={{0,2},{1,3},{2,0},{3,1},{4,6},{5,7},{6,4},{7,5},{8,10},{9,11},{10,... | collective-permute-start | bytes 1769480 | tf_op jit(solution)/shard_map/ppermute | solution.py:26
  138.1 26.5 %collective-permute-start.7 = (bf16[2,2,192,384]{3,2,1,0:T(8,128)(2,1)S(1)}, bf16[2,2,192,384]{3,2,1,0:T(8,128)(2,1)S(1)}, u32[]{:S(2)}, u32[]{:S(2)}) collective-permute-start(bf16[2,2,192,384]{3,2,1,0:T(8,128)(2,1)S(1)} %copy-done.66), channel_id=1, source_target_pairs={{0,2},{1,3},{2,0},{3,1},{4,6},{5,7},{6,4},{7,5},{8,10},{9,11},{10,... | collective-permute-start | bytes 1769480 | tf_op jit(solution)/shard_map/ppermute | solution.py:26
  168.6 22.5 %collective-permute-start.11 = (bf16[2,192,384]{2,1,0:T(8,128)(2,1)}, bf16[2,192,384]{2,1,0:T(8,128)(2,1)S(1)}, u32[]{:S(2)}, u32[]{:S(2)}) collective-permute-start(bf16[2,192,384]{2,1,0:T(8,128)(2,1)} %get-tuple-element.177), channel_id=1, source_target_pairs={{0,4},{1,5},{2,6},{3,7},{4,0},{5,1},{6,2},{7,3},{8,12},{9,13},{10,... | collective-permute-start | bytes 884744 | tf_op jit(solution)/shard_map/ppermute | solution.py:26
  170.5 20.7 %collective-permute-start.12 = (bf16[2,192,384]{2,1,0:T(8,128)(2,1)}, bf16[2,192,384]{2,1,0:T(8,128)(2,1)S(1)}, u32[]{:S(2)}, u32[]{:S(2)}) collective-permute-start(bf16[2,192,384]{2,1,0:T(8,128)(2,1)} %get-tuple-element.178), channel_id=1, source_target_pairs={{0,4},{1,5},{2,6},{3,7},{4,0},{5,1},{6,2},{7,3},{8,12},{9,13},{10,... | collective-permute-start | bytes 884744 | tf_op jit(solution)/shard_map/ppermute | solution.py:26
  170.7 20.5 %collective-permute-start.13 = (bf16[2,2,48,768]{3,2,1,0:T(8,128)(2,1)S(1)}, bf16[2,2,48,768]{3,2,1,0:T(8,128)(2,1)S(1)}, u32[]{:S(2)}, u32[]{:S(2)}) collective-permute-start(bf16[2,2,48,768]{3,2,1,0:T(8,128)(2,1)S(1)} %copy-done.67), channel_id=1, source_target_pairs={{0,4},{1,5},{2,6},{3,7},{4,0},{5,1},{6,2},{7,3},{8,12},{9,13},{10,... | collective-permute-start | bytes 884744 | tf_op jit(solution)/shard_map/ppermute | solution.py:26
  172.5 54.6 %collective-permute-start.15 = (bf16[2,2,48,1536]{3,2,1,0:T(8,128)(2,1)S(1)}, bf16[2,2,48,1536]{3,2,1,0:T(8,128)(2,1)S(1)}, u32[]{:S(2)}, u32[]{:S(2)}) collective-permute-start(bf16[2,2,48,1536]{3,2,1,0:T(8,128)(2,1)S(1)} %copy-done.63), channel_id=1, source_target_pairs={{0,2},{1,3},{2,0},{3,1},{4,6},{5,7},{6,4},{7,5},{8,10},{9,11},{10,... | collective-permute-start | bytes 1769480 | tf_op jit(solution)/shard_map/ppermute | solution.py:26
  174.0 53.5 %collective-permute-start.16 = (bf16[2,2,48,1536]{3,2,1,0:T(8,128)(2,1)S(1)}, bf16[2,2,48,1536]{3,2,1,0:T(8,128)(2,1)S(1)}, u32[]{:S(2)}, u32[]{:S(2)}) collective-permute-start(bf16[2,2,48,1536]{3,2,1,0:T(8,128)(2,1)S(1)} %copy-done.64), channel_id=1, source_target_pairs={{0,2},{1,3},{2,0},{3,1},{4,6},{5,7},{6,4},{7,5},{8,10},{9,11},{10,... | collective-permute-start | bytes 1769480 | tf_op jit(solution)/shard_map/ppermute | solution.py:26
  195.1 29.0 %collective-permute-start.17 = (bf16[192,384]{1,0:T(8,128)(2,1)}, bf16[192,384]{1,0:T(8,128)(2,1)S(1)}, u32[]{:S(2)}, u32[]{:S(2)}) collective-permute-start(bf16[192,384]{1,0:T(8,128)(2,1)} %get-tuple-element.186), channel_id=1, source_target_pairs={{0,8},{1,9},{2,10},{3,11},{4,12},{5,13},{6,14},{7,15},{8,0},{9,1},... | collective-permute-start | bytes 442376 | tf_op jit(solution)/shard_map/ppermute | solution.py:26
  197.7 26.6 %collective-permute-start.18 = (bf16[192,384]{1,0:T(8,128)(2,1)}, bf16[192,384]{1,0:T(8,128)(2,1)S(1)}, u32[]{:S(2)}, u32[]{:S(2)}) collective-permute-start(bf16[192,384]{1,0:T(8,128)(2,1)} %get-tuple-element.187), channel_id=1, source_target_pairs={{0,8},{1,9},{2,10},{3,11},{4,12},{5,13},{6,14},{7,15},{8,0},{9,1},... | collective-permute-start | bytes 442376 | tf_op jit(solution)/shard_map/ppermute | solution.py:26
  198.1 26.7 %collective-permute-start.19 = (bf16[2,48,768]{2,1,0:T(8,128)(2,1)}, bf16[2,48,768]{2,1,0:T(8,128)(2,1)S(1)}, u32[]{:S(2)}, u32[]{:S(2)}) collective-permute-start(bf16[2,48,768]{2,1,0:T(8,128)(2,1)} %get-tuple-element.188), channel_id=1, source_target_pairs={{0,8},{1,9},{2,10},{3,11},{4,12},{5,13},{6,14},{7,15},{8,0},{9,1},... | collective-permute-start | bytes 442376 | tf_op jit(solution)/shard_map/ppermute | solution.py:26
  224.2 13.8 %collective-permute-start.23 = (bf16[8,48,768]{2,1,0:T(8,128)(2,1)}, bf16[8,48,768]{2,1,0:T(8,128)(2,1)S(1)}, u32[]{:S(2)}, u32[]{:S(2)}) collective-permute-start(bf16[8,48,768]{2,1,0:T(8,128)(2,1)} %get-tuple-element.200), channel_id=1, source_target_pairs={{0,1},{1,0},{2,3},{3,2},{4,5},{5,4},{6,7},{7,6},{8,9},{9,8},{10,11... | collective-permute-start | bytes 1769480 | tf_op jit(solution)/shard_map/ppermute | solution.py:26
  224.3 14.5 %collective-permute-start.24 = (bf16[8,48,768]{2,1,0:T(8,128)(2,1)}, bf16[8,48,768]{2,1,0:T(8,128)(2,1)S(1)}, u32[]{:S(2)}, u32[]{:S(2)}) collective-permute-start(bf16[8,48,768]{2,1,0:T(8,128)(2,1)} %get-tuple-element.202), channel_id=1, source_target_pairs={{0,1},{1,0},{2,3},{3,2},{4,5},{5,4},{6,7},{7,6},{8,9},{9,8},{10,11... | collective-permute-start | bytes 1769480 | tf_op jit(solution)/shard_map/ppermute | solution.py:26
  224.8 15.2 %collective-permute-start.25 = (bf16[8,48,768]{2,1,0:T(8,128)(2,1)}, bf16[8,48,768]{2,1,0:T(8,128)(2,1)S(1)}, u32[]{:S(2)}, u32[]{:S(2)}) collective-permute-start(bf16[8,48,768]{2,1,0:T(8,128)(2,1)} %get-tuple-element.204), channel_id=1, source_target_pairs={{0,1},{1,0},{2,3},{3,2},{4,5},{5,4},{6,7},{7,6},{8,9},{9,8},{10,11... | collective-permute-start | bytes 1769480 | tf_op jit(solution)/shard_map/ppermute | solution.py:26
  227.1 5.7 %collective-permute-start.26 = (f32[12,768]{1,0:T(8,128)}, f32[12,768]{1,0:T(8,128)S(1)}, u32[]{:S(2)}, u32[]{:S(2)}) collective-permute-start(f32[12,768]{1,0:T(8,128)} %get-tuple-element.205.refs_6_), channel_id=1, source_target_pairs={{0,1},{1,0},{2,3},{3,2},{4,5},{5,4},{6,7},{7,6},{8,9},{9,8},{10,11... | collective-permute-start | bytes 110600 | tf_op jit(solution)/shard_map/ppermute | solution.py:26
  227.6 60.0 %collective-permute-start.14 = (bf16[8,64,768]{2,1,0:T(8,128)(2,1)}, bf16[8,64,768]{2,1,0:T(8,128)(2,1)S(1)}, u32[]{:S(2)}, u32[]{:S(2)}) collective-permute-start(bf16[8,64,768]{2,1,0:T(8,128)(2,1)} %get-tuple-element.183), channel_id=1, source_target_pairs={{0,16},{16,0},{1,17},{17,1},{2,18},{18,2},{3,19},{19,3},{4,20},{20... | collective-permute-start | bytes 2359304 | tf_op jit(solution)/shard_map/ppermute | solution.py:26
  232.9 4.6 %collective-permute-start.22 = (bf16[48,768]{1,0:T(8,128)(2,1)}, bf16[48,768]{1,0:T(8,128)(2,1)S(1)}, u32[]{:S(2)}, u32[]{:S(2)}) collective-permute-start(bf16[48,768]{1,0:T(8,128)(2,1)} %get-tuple-element.198), channel_id=1, source_target_pairs={{0,2},{1,3},{2,0},{3,1},{4,6},{5,7},{6,4},{7,5},{8,10},{9,11},{10,... | collective-permute-start | bytes 221192 | tf_op jit(solution)/shard_map/ppermute | solution.py:26
  237.5 16.6 %collective-permute-start.20 = (bf16[2,48,1536]{2,1,0:T(8,128)(2,1)}, bf16[2,48,1536]{2,1,0:T(8,128)(2,1)S(1)}, u32[]{:S(2)}, u32[]{:S(2)}) collective-permute-start(bf16[2,48,1536]{2,1,0:T(8,128)(2,1)} %get-tuple-element.196), channel_id=1, source_target_pairs={{0,4},{1,5},{2,6},{3,7},{4,0},{5,1},{6,2},{7,3},{8,12},{9,13},{10,... | collective-permute-start | bytes 884744 | tf_op jit(solution)/shard_map/ppermute | solution.py:26
  238.0 13.3 %collective-permute-start.33 = (bf16[192,384]{1,0:T(8,128)(2,1)}, bf16[192,384]{1,0:T(8,128)(2,1)S(1)}, u32[]{:S(2)}, u32[]{:S(2)}) collective-permute-start(bf16[192,384]{1,0:T(8,128)(2,1)} %get-tuple-element.214.refs_0_), channel_id=1, source_target_pairs={{0,16},{16,0},{1,17},{17,1},{2,18},{18,2},{3,19},{19,3},{4,20},{20... | collective-permute-start | bytes 442376 | tf_op jit(solution)/shard_map/ppermute | solution.py:26
  238.8 14.9 %collective-permute-start.34 = (bf16[192,384]{1,0:T(8,128)(2,1)}, bf16[192,384]{1,0:T(8,128)(2,1)S(1)}, u32[]{:S(2)}, u32[]{:S(2)}) collective-permute-start(bf16[192,384]{1,0:T(8,128)(2,1)} %get-tuple-element.215.refs_2_), channel_id=1, source_target_pairs={{0,16},{16,0},{1,17},{17,1},{2,18},{18,2},{3,19},{19,3},{4,20},{20... | collective-permute-start | bytes 442376 | tf_op jit(solution)/shard_map/ppermute | solution.py:26
  240.0 15.6 %collective-permute-start.21 = (bf16[2,48,1536]{2,1,0:T(8,128)(2,1)}, bf16[2,48,1536]{2,1,0:T(8,128)(2,1)S(1)}, u32[]{:S(2)}, u32[]{:S(2)}) collective-permute-start(bf16[2,48,1536]{2,1,0:T(8,128)(2,1)} %get-tuple-element.197), channel_id=1, source_target_pairs={{0,4},{1,5},{2,6},{3,7},{4,0},{5,1},{6,2},{7,3},{8,12},{9,13},{10,... | collective-permute-start | bytes 884744 | tf_op jit(solution)/shard_map/ppermute | solution.py:26
  251.3 15.3 %collective-permute-start.29 = (bf16[2,2,48,768]{3,2,1,0:T(8,128)(2,1)}, bf16[2,2,48,768]{3,2,1,0:T(8,128)(2,1)S(1)}, u32[]{:S(2)}, u32[]{:S(2)}) collective-permute-start(bf16[2,2,48,768]{3,2,1,0:T(8,128)(2,1)} %get-tuple-element.210), channel_id=1, source_target_pairs={{0,2},{1,3},{2,0},{3,1},{4,6},{5,7},{6,4},{7,5},{8,10},{9,11},{10,... | collective-permute-start | bytes 884744 | tf_op jit(solution)/shard_map/ppermute | solution.py:26
  253.6 18.2 %collective-permute-start.30 = (bf16[2,2,48,768]{3,2,1,0:T(8,128)(2,1)}, bf16[2,2,48,768]{3,2,1,0:T(8,128)(2,1)S(1)}, u32[]{:S(2)}, u32[]{:S(2)}) collective-permute-start(bf16[2,2,48,768]{3,2,1,0:T(8,128)(2,1)} %get-tuple-element.211), channel_id=1, source_target_pairs={{0,4},{1,5},{2,6},{3,7},{4,0},{5,1},{6,2},{7,3},{8,12},{9,13},{10,... | collective-permute-start | bytes 884744 | tf_op jit(solution)/shard_map/ppermute | solution.py:26
  254.1 17.7 %collective-permute-start.31 = (bf16[2,2,48,768]{3,2,1,0:T(8,128)(2,1)}, bf16[2,2,48,768]{3,2,1,0:T(8,128)(2,1)S(1)}, u32[]{:S(2)}, u32[]{:S(2)}) collective-permute-start(bf16[2,2,48,768]{3,2,1,0:T(8,128)(2,1)} %get-tuple-element.212), channel_id=1, source_target_pairs={{0,2},{1,3},{2,0},{3,1},{4,6},{5,7},{6,4},{7,5},{8,10},{9,11},{10,... | collective-permute-start | bytes 884744 | tf_op jit(solution)/shard_map/ppermute | solution.py:26
  255.7 10.6 %collective-permute-start.32 = (f32[12,768]{1,0:T(8,128)}, f32[12,768]{1,0:T(8,128)S(1)}, u32[]{:S(2)}, u32[]{:S(2)}) collective-permute-start(f32[12,768]{1,0:T(8,128)} %get-tuple-element.213.refs_9_), channel_id=1, source_target_pairs={{0,2},{1,3},{2,0},{3,1},{4,6},{5,7},{6,4},{7,5},{8,10},{9,11},{10,... | collective-permute-start | bytes 110600 | tf_op jit(solution)/shard_map/ppermute | solution.py:26
  266.2 13.3 %collective-permute-start.27 = (bf16[48,1536]{1,0:T(8,128)(2,1)}, bf16[48,1536]{1,0:T(8,128)(2,1)S(1)}, u32[]{:S(2)}, u32[]{:S(2)}) collective-permute-start(bf16[48,1536]{1,0:T(8,128)(2,1)} %get-tuple-element.208), channel_id=1, source_target_pairs={{0,8},{1,9},{2,10},{3,11},{4,12},{5,13},{6,14},{7,15},{8,0},{9,1},... | collective-permute-start | bytes 442376 | tf_op jit(solution)/shard_map/ppermute | solution.py:26
  266.6 17.2 %collective-permute-start.28 = (bf16[48,1536]{1,0:T(8,128)(2,1)}, bf16[48,1536]{1,0:T(8,128)(2,1)S(1)}, u32[]{:S(2)}, u32[]{:S(2)}) collective-permute-start(bf16[48,1536]{1,0:T(8,128)(2,1)} %get-tuple-element.209), channel_id=1, source_target_pairs={{0,8},{1,9},{2,10},{3,11},{4,12},{5,13},{6,14},{7,15},{8,0},{9,1},... | collective-permute-start | bytes 442376 | tf_op jit(solution)/shard_map/ppermute | solution.py:26
  275.6 16.5 %collective-permute-start.35 = (bf16[2,48,768]{2,1,0:T(8,128)(2,1)}, bf16[2,48,768]{2,1,0:T(8,128)(2,1)S(1)}, u32[]{:S(2)}, u32[]{:S(2)}) collective-permute-start(bf16[2,48,768]{2,1,0:T(8,128)(2,1)} %get-tuple-element.221), channel_id=1, source_target_pairs={{0,4},{1,5},{2,6},{3,7},{4,0},{5,1},{6,2},{7,3},{8,12},{9,13},{10,... | collective-permute-start | bytes 442376 | tf_op jit(solution)/shard_map/ppermute | solution.py:26
  276.1 21.8 %collective-permute-start.36 = (bf16[2,48,768]{2,1,0:T(8,128)(2,1)}, bf16[2,48,768]{2,1,0:T(8,128)(2,1)S(1)}, u32[]{:S(2)}, u32[]{:S(2)}) collective-permute-start(bf16[2,48,768]{2,1,0:T(8,128)(2,1)} %get-tuple-element.222), channel_id=1, source_target_pairs={{0,8},{1,9},{2,10},{3,11},{4,12},{5,13},{6,14},{7,15},{8,0},{9,1},... | collective-permute-start | bytes 442376 | tf_op jit(solution)/shard_map/ppermute | solution.py:26
  279.5 18.4 %collective-permute-start.37 = (bf16[2,48,768]{2,1,0:T(8,128)(2,1)}, bf16[2,48,768]{2,1,0:T(8,128)(2,1)S(1)}, u32[]{:S(2)}, u32[]{:S(2)}) collective-permute-start(bf16[2,48,768]{2,1,0:T(8,128)(2,1)} %get-tuple-element.223), channel_id=1, source_target_pairs={{0,4},{1,5},{2,6},{3,7},{4,0},{5,1},{6,2},{7,3},{8,12},{9,13},{10,... | collective-permute-start | bytes 442376 | tf_op jit(solution)/shard_map/ppermute | solution.py:26
  283.8 6.8 %collective-permute-start.38 = (f32[12,768]{1,0:T(8,128)}, f32[12,768]{1,0:T(8,128)S(1)}, u32[]{:S(2)}, u32[]{:S(2)}) collective-permute-start(f32[12,768]{1,0:T(8,128)} %get-tuple-element.224.refs_12_), channel_id=1, source_target_pairs={{0,4},{1,5},{2,6},{3,7},{4,0},{5,1},{6,2},{7,3},{8,12},{9,13},{10,... | collective-permute-start | bytes 110600 | tf_op jit(solution)/shard_map/ppermute | solution.py:26
  287.6 18.2 %collective-permute-start.43 = (bf16[48,1536]{1,0:T(8,128)(2,1)}, bf16[48,1536]{1,0:T(8,128)(2,1)S(1)}, u32[]{:S(2)}, u32[]{:S(2)}) collective-permute-start(bf16[48,1536]{1,0:T(8,128)(2,1)} %get-tuple-element.230.refs_0_), channel_id=1, source_target_pairs={{0,16},{16,0},{1,17},{17,1},{2,18},{18,2},{3,19},{19,3},{4,20},{20... | collective-permute-start | bytes 442376 | tf_op jit(solution)/shard_map/ppermute | solution.py:26
  290.6 17.5 %collective-permute-start.44 = (bf16[48,1536]{1,0:T(8,128)(2,1)}, bf16[48,1536]{1,0:T(8,128)(2,1)S(1)}, u32[]{:S(2)}, u32[]{:S(2)}) collective-permute-start(bf16[48,1536]{1,0:T(8,128)(2,1)} %get-tuple-element.231.refs_2_), channel_id=1, source_target_pairs={{0,16},{16,0},{1,17},{17,1},{2,18},{18,2},{3,19},{19,3},{4,20},{20... | collective-permute-start | bytes 442376 | tf_op jit(solution)/shard_map/ppermute | solution.py:26
  292.1 10.8 %collective-permute-start.45 = (bf16[48,768]{1,0:T(8,128)(2,1)S(1)}, bf16[48,768]{1,0:T(8,128)(2,1)S(1)}, u32[]{:S(2)}, u32[]{:S(2)}) collective-permute-start(bf16[48,768]{1,0:T(8,128)(2,1)S(1)} %copy-done.51), channel_id=1, source_target_pairs={{0,16},{16,0},{1,17},{17,1},{2,18},{18,2},{3,19},{19,3},{4,20},{20... | collective-permute-start | bytes 221192 | tf_op jit(solution)/shard_map/ppermute | solution.py:26
  301.3 10.2 %collective-permute-start.39 = (bf16[48,768]{1,0:T(8,128)(2,1)}, bf16[48,768]{1,0:T(8,128)(2,1)S(1)}, u32[]{:S(2)}, u32[]{:S(2)}) collective-permute-start(bf16[48,768]{1,0:T(8,128)(2,1)} %get-tuple-element.226), channel_id=1, source_target_pairs={{0,8},{1,9},{2,10},{3,11},{4,12},{5,13},{6,14},{7,15},{8,0},{9,1},... | collective-permute-start | bytes 221192 | tf_op jit(solution)/shard_map/ppermute | solution.py:26
  301.3 10.2 %collective-permute-start.40 = (bf16[48,768]{1,0:T(8,128)(2,1)}, bf16[48,768]{1,0:T(8,128)(2,1)S(1)}, u32[]{:S(2)}, u32[]{:S(2)}) collective-permute-start(bf16[48,768]{1,0:T(8,128)(2,1)} %get-tuple-element.227), channel_id=1, source_target_pairs={{0,2},{1,3},{2,0},{3,1},{4,6},{5,7},{6,4},{7,5},{8,10},{9,11},{10,... | collective-permute-start | bytes 221192 | tf_op jit(solution)/shard_map/ppermute | solution.py:26
  302.9 8.6 %collective-permute-start.41 = (bf16[48,768]{1,0:T(8,128)(2,1)}, bf16[48,768]{1,0:T(8,128)(2,1)S(1)}, u32[]{:S(2)}, u32[]{:S(2)}) collective-permute-start(bf16[48,768]{1,0:T(8,128)(2,1)} %get-tuple-element.228), channel_id=1, source_target_pairs={{0,8},{1,9},{2,10},{3,11},{4,12},{5,13},{6,14},{7,15},{8,0},{9,1},... | collective-permute-start | bytes 221192 | tf_op jit(solution)/shard_map/ppermute | solution.py:26
  305.7 5.7 %collective-permute-start.42 = (f32[12,768]{1,0:T(8,128)}, f32[12,768]{1,0:T(8,128)S(1)}, u32[]{:S(2)}, u32[]{:S(2)}) collective-permute-start(f32[12,768]{1,0:T(8,128)} %get-tuple-element.229.refs_15_), channel_id=1, source_target_pairs={{0,8},{1,9},{2,10},{3,11},{4,12},{5,13},{6,14},{7,15},{8,0},{9,1},... | collective-permute-start | bytes 110600 | tf_op jit(solution)/shard_map/ppermute | solution.py:26
  314.9 7.9 %collective-permute-start.46 = (bf16[48,768]{1,0:T(8,128)(2,1)}, bf16[48,768]{1,0:T(8,128)(2,1)S(1)}, u32[]{:S(2)}, u32[]{:S(2)}) collective-permute-start(bf16[48,768]{1,0:T(8,128)(2,1)} %get-tuple-element.236.refs_0_), channel_id=1, source_target_pairs={{0,16},{16,0},{1,17},{17,1},{2,18},{18,2},{3,19},{19,3},{4,20},{20... | collective-permute-start | bytes 221192 | tf_op jit(solution)/shard_map/ppermute | solution.py:26
  316.4 6.3 %collective-permute-start.47 = (bf16[48,768]{1,0:T(8,128)(2,1)}, bf16[48,768]{1,0:T(8,128)(2,1)S(1)}, u32[]{:S(2)}, u32[]{:S(2)}) collective-permute-start(bf16[48,768]{1,0:T(8,128)(2,1)} %get-tuple-element.237.refs_2_), channel_id=1, source_target_pairs={{0,16},{16,0},{1,17},{17,1},{2,18},{18,2},{3,19},{19,3},{4,20},{20... | collective-permute-start | bytes 221192 | tf_op jit(solution)/shard_map/ppermute | solution.py:26
  317.0 5.8 %collective-permute-start.48 = (bf16[48,768]{1,0:T(8,128)(2,1)}, bf16[48,768]{1,0:T(8,128)(2,1)S(1)}, u32[]{:S(2)}, u32[]{:S(2)}) collective-permute-start(bf16[48,768]{1,0:T(8,128)(2,1)} %get-tuple-element.238.refs_4_), channel_id=1, source_target_pairs={{0,16},{16,0},{1,17},{17,1},{2,18},{18,2},{3,19},{19,3},{4,20},{20... | collective-permute-start | bytes 221192 | tf_op jit(solution)/shard_map/ppermute | solution.py:26
  (70 other events, 354.6 us)
